TPU v7x, 256 devices: a whole 4x4x8 slice. The times are simulated.
256 devices in a mesh: prow: 8 (over z_lo, y), pcol: 32 (over z_hi, x, core).
Axes of the slice: x: 4, y: 4, z: 8 (z_hi: 4, z_lo: 2; z = z_hi * 2 + z_lo), core: 2. Of those that a mesh axis runs over, the one named last changes fastest.
Arguments:
- matrix: float32 [8192, 24576], P('prow', 'pcol'), may hold values from -9 to 9, as said below
- pivot_rows: int32 [128], replicated, may hold values from 128 to 8191, as said below
Outputs:
- factored: float32 [8192, 24576], P('prow', 'pcol')
Inputs may be any that keep to these rules, and one draw needn't show every extreme that they name: `matrix`: columns 0 to 127 hold a factored panel: in global rows 0 to 127 the strictly lower part is the unit lower factor and the rest the upper factor; in all other rows the multipliers, of magnitude at most 1. `pivot_rows`: 128 distinct global rows, none of them among rows 0 to 127.
All inputs are finite; a program needn't handle non-finite values.
Results may differ from a plain program's by a relative error of at most 0.000065.
Values sent between devices are 32-bit elements; how exact they have to be, the bound alone decides.
No kernel may reach another device: no remote copies, remote signals or barrier semaphores. Data moves between devices by JAX's collectives and lax.ppermute only.
A program may use at most 64 MiB of HBM per device.

v0:
```python
import jax
import jax.numpy as jnp
from jax import lax
from jax.sharding import PartitionSpec as P


def spread(shard, axis, root):
    mine = lax.axis_index(axis) == root
    return lax.psum(jnp.where(mine, shard, jnp.zeros_like(shard)), axis)


def make_lower(block):
    return jnp.tril(block, -1) + jnp.eye(block.shape[0], dtype=jnp.float32)


def local(matrix, pivot_rows):
    panel_width = pivot_rows.shape[0]
    row_count = matrix.shape[0]
    row_devices = lax.axis_size("prow")
    my_row = lax.axis_index("prow")
    my_col = lax.axis_index("pcol")
    owners = pivot_rows // panel_width % row_devices
    local_rows = pivot_rows // (panel_width * row_devices) * panel_width + pivot_rows % panel_width
    is_owned = owners == my_row
    picked = jnp.where(
        is_owned[:, None], jnp.take(matrix, jnp.where(is_owned, local_rows, 0), axis=0), 0.0
    )
    on_top = my_row == 0
    old_block = matrix[:panel_width]
    pivot_sum = lax.psum(picked, "prow")
    displaced = spread(old_block, "prow", 0)
    targets = jnp.where(is_owned, local_rows, row_count)
    swapped = matrix.at[targets].set(displaced, mode="drop")
    own_panel = matrix[:, :panel_width]
    panel_block = spread(own_panel, "pcol", 0)
    lower_block = make_lower(spread(panel_block[:panel_width], "prow", 0))
    solved = jax.scipy.linalg.solve_triangular(
        lower_block, pivot_sum, lower=True, unit_diagonal=True
    )
    updated = swapped - jnp.dot(panel_block, solved, precision=lax.Precision.HIGHEST)
    updated = updated.at[:panel_width].set(jnp.where(on_top, solved, updated[:panel_width]))
    updated = updated.at[:, :panel_width].set(
        jnp.where(my_col == 0, own_panel, updated[:, :panel_width])
    )
    return updated


def solution(mesh):
    placed = (P("prow", "pcol"), P())
    return jax.shard_map(
        local, mesh=mesh, in_specs=placed, out_specs=P("prow", "pcol"), check_vma=False
    )
```

profile of v0, /device:TPU:1, one launch (start us, length us, event | category | flops | bytes accessed | tf_op | source)
XLA Modules:
  0.0 408.1 jit_solution(13280406452584330399)
XLA Ops:
  6.5 0.0 all-reduce.4.cloned.1.call-start
  6.5 1.9 slice_select_fusion
  8.4 0.0 all-reduce.4.cloned.1.call-update
  8.4 0.0 all-reduce.6.cloned.1.call-start
  8.5 0.7 compare_and_fusion
  9.2 2.9 gather_fusion
  12.0 2.0 select_select_fusion.1
  14.0 284.6 %all-reduce.4.cloned.1.call-done = f32[1024,128]{1,0:T(8,128)} async-done(((f32[1024,128]{1,0:T(8,128)}), f32[1024,128]{1,0:T(8,128)}) %all-reduce.4.cloned.1.call-update) | async-done | bytes 524304 | tf_op jit(solution)/shard_map/psum | solution.py:9
  298.7 1.5 slice_select_fusion.3
  300.1 0.0 all-reduce.6.cloned.1.call-update
  300.2 1.9 copy.7
  302.0 0.6 compare_reduce_fusion
  302.7 74.7 %all-reduce.6.cloned.1.call-done = (f32[128,768]{1,0:T(8,128)}, f32[128,768]{1,0:T(8,128)}, f32[128,128]{1,0:T(8,128)}) async-done(((f32[128,768]{1,0:T(8,128)}, f32[128,768]{1,0:T(8,128)}, f32[128,128]{1,0:T(8,128)}), (f32[128,768]{1,0:T(8,128)}, f32[128,768]{1,0:T(8,128)}, f32[128,128]{1,0:T(8,128)})) %all-reduce.6.cloned.1.call-update) | async-done | bytes 851984 | tf_op jit(solution)/shard_map/psum | solution.py:9
  377.4 0.9 add_bitcast_fusion
  378.3 10.4 %custom-call.4 = f32[1,128,128]{1,2,0:T(8,128)} custom-call(f32[1,128,128]{2,1,0:T(8,128)S(1)} %add_bitcast_fusion), custom_call_target="InvertDiagBlocksLowerTriangular" | custom-call | tf_op jit(solution)/shard_map/jit(_solve_triangular)/triangular_solve | solution.py:37
  388.7 1.5 fusion.2
  390.3 2.7 scatter_fusion
  393.0 3.9 convolution_subtract_fusion
  396.8 0.1 fusion.1
  396.9 0.0 copy-start
  396.9 1.7 copy-done
  398.6 2.7 fusion
  (3 shorter events, 0.0 us)
Async XLA Ops:
  6.5 292.1 %all-reduce.4.cloned.1.call-start = ((), (), s32[]{:S(2)}) async-start(), calls=%async_computation | async-start | bytes 1048576 | tf_op jit(solution)/shard_map/psum | solution.py:9
  8.4 368.9 %all-reduce.6.cloned.1.call-start = ((), (), s32[]{:S(2)}) async-start(), calls=%async_computation.1 | async-start | bytes 1703936 | tf_op jit(solution)/shard_map/psum | solution.py:9
  396.9 1.7 copy-start
Sparse Core Ops, SparseCore 0:
  10.0 288.6 all-reduce.3
  301.8 75.5 all-reduce.5
where the time goes:
time: 413 us; the launch traced here: 408 us
  waiting for transfers between devices  359 us (87%)
  other arithmetic  20.8 us (5%)
  between operations  13.5 us (3%)
  local copies, waits for them, and re-layouts  9.08 us (2%)
  matrix products  5.39 us (1%)
    psum x2, waiting for transfers between devices, spread(): return lax.psum(jnp.where(mine, shard, jnp.zeros_like(shard)), axis)  359 us
    another operation x3, other arithmetic, local(): jax.scipy.linalg.solve_triangular(lower_block, pivot_sum, lower=True, uni...  11.4 us
  transfers between devices with their start and end apart: 2, of which 2 were waited for; matrix products, arithmetic and copies ran while one was open for 2% of the time, Pallas kernels for 0%

commit v1 on v0

v1 whole, which is shorter than its diff:
```python
import functools

import jax
import jax.numpy as jnp
from jax import lax
from jax.experimental import pallas as pl
from jax.experimental.pallas import tpu as pltpu
from jax.sharding import Mesh, PartitionSpec as P

NB = 128
EXACT = lax.Precision.HIGHEST
ROWS = ("zl", "y")
COLS = ("zh", "x", "c")
N_Y, N_X, N_ZH, N_C = 4, 4, 4, 2
N_PROW = 8


def prow_id(zl, y):
    return zl * N_Y + y


def pcol_id(zh, x, c):
    return (zh * N_X + x) * N_C + c


def owned_row(pivot, my_row):
    is_owned = ((pivot >> 7) & (N_PROW - 1)) == my_row
    return is_owned, ((pivot >> 10) << 7) + (pivot & (NB - 1))


def pick_kernel(pivots, my_row, matrix, out):
    cols = matrix.shape[1]
    step = NB // N_PROW
    on_top = my_row[0] == 0

    def body(j, _):
        for i in range(step):
            is_owned, row = owned_row(pivots[j * step + i], my_row[0])
            got = matrix[pl.ds(jnp.where(is_owned, row, 0), 1), :]
            out[j, pl.ds(i, 1), :] = jnp.where(is_owned, got, 0.0)
        top = matrix[pl.ds(pl.multiple_of(j * step, step), step), :]
        out[j, step:, :] = jnp.where(on_top, top, 0.0)
        return 0

    lax.fori_loop(0, N_PROW, body, 0)


def pick(pivots, my_row, matrix):
    cols = matrix.shape[1]
    return pl.pallas_call(
        pick_kernel,
        out_shape=jax.ShapeDtypeStruct((N_PROW, 2 * NB // N_PROW, cols), jnp.float32),
        grid_spec=pltpu.PrefetchScalarGridSpec(
            num_scalar_prefetch=2,
            grid=(1,),
            in_specs=[pl.BlockSpec(matrix.shape, lambda i, *_: (0, 0))],
            out_specs=pl.BlockSpec(
                (N_PROW, 2 * NB // N_PROW, cols), lambda i, *_: (0, 0, 0)
            ),
        ),
        compiler_params=pltpu.CompilerParams(vmem_limit_bytes=32 << 20),
        name="pick",
    )(pivots, my_row, matrix)


def invert_kernel(block, out):
    rows = lax.broadcasted_iota(jnp.int32, (NB, NB), 0)
    cols = lax.broadcasted_iota(jnp.int32, (NB, NB), 1)
    lower = block[...]
    inverse = jnp.where(rows == cols, 1.0, 0.0)
    size = 1
    while size < NB:
        shift = size.bit_length()
        same = (rows >> shift) == (cols >> shift)
        below = ((rows & size) != 0) & ((cols & size) == 0)
        part = jnp.where(same & below, lower, 0.0)
        if size == 1:
            inverse = inverse - part
        else:
            half = jnp.dot(part, inverse, precision=EXACT, preferred_element_type=jnp.float32)
            inverse = inverse - jnp.dot(
                inverse, half, precision=EXACT, preferred_element_type=jnp.float32
            )
        size *= 2
    out[...] = inverse


def invert(block):
    return pl.pallas_call(
        invert_kernel,
        out_shape=jax.ShapeDtypeStruct((NB, NB), jnp.float32),
        name="invert",
    )(block)


def solve_kernel(pivots, my_row, matrix, inverse, rows, swapped, solved):
    step = NB // N_PROW
    picked = rows[:, :step, :].reshape(NB, rows.shape[-1])
    solved[...] = jnp.dot(
        inverse[...], picked, precision=EXACT, preferred_element_type=jnp.float32
    )
    swapped[...] = matrix[...]

    def body(j, _):
        for i in range(step):
            is_owned, row = owned_row(pivots[j * step + i], my_row[0])

            @pl.when(is_owned)
            def _():
                swapped[pl.ds(row, 1), :] = rows[j, pl.ds(step + i, 1), :]

        return 0

    lax.fori_loop(0, N_PROW, body, 0)


def solve(pivots, my_row, matrix, inverse, rows):
    whole = lambda a: pl.BlockSpec(a.shape, lambda i, *_: (0,) * a.ndim)
    return pl.pallas_call(
        solve_kernel,
        out_shape=(
            jax.ShapeDtypeStruct(matrix.shape, jnp.float32),
            jax.ShapeDtypeStruct((NB, matrix.shape[1]), jnp.float32),
        ),
        grid_spec=pltpu.PrefetchScalarGridSpec(
            num_scalar_prefetch=2,
            grid=(1,),
            in_specs=[whole(matrix), whole(inverse), whole(rows)],
            out_specs=(
                pl.BlockSpec(matrix.shape, lambda i, *_: (0, 0)),
                pl.BlockSpec((NB, matrix.shape[1]), lambda i, *_: (0, 0)),
            ),
        ),
        compiler_params=pltpu.CompilerParams(vmem_limit_bytes=48 << 20),
        name="solve",
    )(pivots, my_row, matrix, inverse, rows)


def update_kernel(place, panel, solved, swapped, out):
    step = pl.program_id(0)
    piece = panel[0]
    out[...] = swapped[...] - jnp.dot(
        piece, solved[...], precision=EXACT, preferred_element_type=jnp.float32
    )
    first = ((place[1] + N_X - step) & (N_X - 1)) == 0

    @pl.when((place[0] == 0) & first)
    def _():
        out[:NB, :] = solved[...]

    @pl.when(place[2] == 0)
    def _():
        out[:, :NB] = piece


def update(place, panel, solved, swapped):
    parts, height, _ = panel.shape
    cols = swapped.shape[1]
    block = lambda i, place: ((place[1] + N_X - i) & (N_X - 1), 0)
    return pl.pallas_call(
        update_kernel,
        out_shape=jax.ShapeDtypeStruct(swapped.shape, jnp.float32),
        grid_spec=pltpu.PrefetchScalarGridSpec(
            num_scalar_prefetch=1,
            grid=(parts,),
            in_specs=[
                pl.BlockSpec((1, height, NB), lambda i, place: (i, 0, 0)),
                pl.BlockSpec(solved.shape, lambda i, place: (0, 0)),
                pl.BlockSpec((height, cols), block),
            ],
            out_specs=pl.BlockSpec((height, cols), block),
        ),
        compiler_params=pltpu.CompilerParams(vmem_limit_bytes=48 << 20),
        name="update",
    )(place, panel, solved, swapped)


def local(matrix, pivot_rows):
    height = matrix.shape[0] // N_X
    zl, y = lax.axis_index("zl"), lax.axis_index("y")
    zh, x, c = (lax.axis_index(name) for name in COLS)
    my_row = prow_id(zl, y)
    my_col = pcol_id(zh, x, c)
    row_arg = my_row.reshape(1).astype(jnp.int32)
    place = jnp.stack([my_row, x, my_col]).astype(jnp.int32)

    top = matrix[:NB, :NB]
    lower = top
    origin = my_row == 0
    for pairs in (
        [(prow_id(0, 0), prow_id(1, 0))],
        [(prow_id(a, 0), prow_id(a, 1)) for a in (0, 1)],
        [(prow_id(a, b), prow_id(a, (3, 2)[b])) for a in (0, 1) for b in (0, 1)],
    ):
        whole = [(s * 32, t * 32) for s, t in pairs]
        got = lax.ppermute(lower, ROWS + COLS, whole)
        is_target = functools.reduce(
            jnp.logical_or, [my_row == t for _, t in pairs], jnp.bool_(False)
        )
        lower = jnp.where(is_target, got, lower)

    quarter = matrix[:height, :NB]
    for k in range(1, N_X):
        piece = matrix[k * height : (k + 1) * height, :NB]
        got = lax.ppermute(piece, COLS, [(0, pcol_id(0, k, 0))])
        quarter = jnp.where(x == k, got, quarter)

    sent = pick(pivot_rows, row_arg, matrix)
    got = lax.all_to_all(sent, ROWS, 0, 0)
    mine = jnp.sum(got, axis=0)
    rows = lax.all_to_all(
        jnp.broadcast_to(mine[None], (N_PROW,) + mine.shape), ROWS, 0, 0
    )

    held = jnp.concatenate([quarter, lower], axis=0)
    down = held
    for k in range(1, N_ZH):
        got = lax.ppermute(
            held, COLS, [(pcol_id(0, a, 0), pcol_id(k, a, 0)) for a in range(N_X)]
        )
        down = jnp.where(zh == k, got, down)

    pieces = [down[:height]]
    lower = down[height:]
    for k in range(1, N_X):
        got = lax.ppermute(
            down,
            COLS,
            [
                (pcol_id(b, a, 0), pcol_id(b, (a + k) % N_X, 0))
                for a in range(N_X)
                for b in range(N_ZH)
            ],
        )
        pieces.append(got[:height])
        lower = jnp.where(x == k, got[height:], lower)

    held = jnp.concatenate(pieces + [lower], axis=0)
    got = lax.ppermute(
        held,
        COLS,
        [(pcol_id(b, a, 0), pcol_id(b, a, 1)) for a in range(N_X) for b in range(N_ZH)],
    )
    held = jnp.where(c == 1, got, held)
    panel = held[: N_X * height].reshape(N_X, height, NB)
    inverse = invert(held[N_X * height :])
    swapped, solved = solve(pivot_rows, row_arg, matrix, inverse, rows)
    return update(place, panel, solved, swapped)


def solution(mesh):
    fine = Mesh(mesh.devices.reshape(2, N_Y, N_ZH, N_X, N_C), ROWS + COLS)
    placed = (P(ROWS, COLS), P())
    return jax.shard_map(
        local, mesh=fine, in_specs=placed, out_specs=P(ROWS, COLS), check_vma=False
    )
```

time: 413 us -> 80.8 us (0.20)
  waiting for transfers between devices: 359 us -> 36.1 us
  starting transfers between devices: 0.04 us -> 19.2 us
  other arithmetic: 20.8 us -> 2.06 us
  Pallas kernels: 0 us -> 15.4 us
  between operations: 13.5 us -> 0.35 us
  matrix products: 5.39 us -> 0 us
    psum x2 -> x0, waiting for transfers between devices: 359 us -> none  [spread(): return lax.psum(jnp.where(mine, shard, jnp.zeros_like(shard)), axis)]
    ppermute x0 -> x13, waiting for transfers between devices: none -> 33.7 us  [the longest x1 33.7 us: local(): lax.ppermute(held, COLS, [(pcol_id(b, a, 0), pcol_id(b, a, 1)) for a in r...]
    pallas_call x0 -> x4, Pallas kernels: none -> 15.4 us  [the longest x1 4.71 us: update(): pl.pallas_call(update_kernel, out_shape=jax.ShapeDtypeStruct(swapped.shap...]
    another operation x4 -> x1, other arithmetic: 12 us -> 0.08 us  [local(): place = jnp.stack([my_row, x, my_col]).astype(jnp.int32)]
    all_to_all x0 -> x2, starting transfers between devices: none -> 9.92 us  [the longest x1 6.37 us: local(): got = lax.all_to_all(sent, ROWS, 0, 0)]
    ppermute x0 -> x13, starting transfers between devices: none -> 9.32 us  [the longest x3 2.02 us: local(): lax.ppermute(held, COLS, [(pcol_id(0, a, 0), pcol_id(k, a, 0)) for a in r...]
  transfers between devices with their start and end apart: 2 -> 15, of which waited for: 2 -> 2; matrix products, arithmetic and copies ran while one was open for 2% -> 5% of each run, Pallas kernels for 0% -> 8%
where the time goes in v1:
time: 80.8 us; the launch traced here: 80 us
  waiting for transfers between devices  36.1 us (45%)
  starting transfers between devices  19.2 us (24%)
  Pallas kernels  15.4 us (19%)
  local copies, waits for them, and re-layouts  6.93 us (9%)
  other arithmetic  2.06 us (3%)
    ppermute x1, waiting for transfers between devices, local(): lax.ppermute(held, COLS, [(pcol_id(b, a, 0), pcol_id(b, a, 1)) for a in r...  33.7 us
    all_to_all x1, starting transfers between devices, local(): got = lax.all_to_all(sent, ROWS, 0, 0)  6.37 us
    pallas_call x1, Pallas kernels, update(): pl.pallas_call(update_kernel, out_shape=jax.ShapeDtypeStruct(swapped.shap...  4.71 us
    pallas_call x1, Pallas kernels, solve(): pl.pallas_call(solve_kernel, out_shape=(jax.ShapeDtypeStruct(matrix.shape...  4.42 us
    pallas_call x1, Pallas kernels, invert(): pl.pallas_call(invert_kernel, out_shape=jax.ShapeDtypeStruct((NB, NB), jn...  4.13 us
    all_to_all x1, starting transfers between devices, local(): lax.all_to_all(jnp.broadcast_to(mine[None], (N_PROW,) + mine.shape), ROWS...  3.55 us
    unnamed x12, local copies, waits for them, and re-layouts  3.43 us
    all_to_all x1, waiting for transfers between devices, local(): got = lax.all_to_all(sent, ROWS, 0, 0)  2.36 us
  transfers between devices with their start and end apart: 15, of which 2 were waited for; matrix products, arithmetic and copies ran while one was open for 5% of the time, Pallas kernels for 8%

profile of v1, /device:TPU:1, one launch (start us, length us, event | category | flops | bytes accessed | tf_op | source)
XLA Modules:
  0.0 80.0 jit_solution(9339421330372557340)
XLA Ops:
  0.0 0.8 %slice.49 = f32[128,128]{1,0:T(8,128)S(1)} slice(f32[1024,768]{1,0:T(8,128)} %matrix.3), slice={[0:128], [0:128]} | slice | bytes 131072 | tf_op jit(solution)/shard_map/slice | solution.py:187
  1.5 0.9 %broadcast_select_fusion.1 = f32[128,128]{1,0:T(8,128)S(1)} fusion(f32[128,128]{1,0:T(8,128)S(1)} %collective-permute-done.3, pred[]{:T(512)S(6)} %eq.56, f32[1024,768]{1,0:T(8,128)} %matrix.3), kind=kLoop, calls=%fused_computation.12 | loop fusion | flops 16384 | bytes 196609 | tf_op jit(solution)/shard_map/jit(_where)/select_n | solution.py:200
  3.0 1.1 %fusion.3 = (f32[256,128]{1,0:T(8,128)S(1)}, f32[256,128]{1,0:T(8,128)S(1)}, f32[256,128]{1,0:T(8,128)S(1)}) fusion(f32[1024,768]{1,0:T(8,128)} %matrix.3), kind=kLoop, calls=%fused_computation.16 | loop fusion | bytes 786432 | tf_op jit(solution)/shard_map/slice | solution.py:204
  4.1 0.7 collective-permute-start.2
  5.5 0.7 collective-permute-start
  6.2 1.9 %copy-done = f32[1024,768]{1,0:T(8,128)S(1)} copy-done((f32[1024,768]{1,0:T(8,128)S(1)}, f32[1024,768]{1,0:T(8,128)}, u32[]{:S(2)}) %copy-start) | copy-done | bytes 3145752
  8.7 2.1 %pick.1 = f32[8,32,768]{2,1,0:T(8,128)} custom-call(s32[128]{0:T(128)S(1)} %copy-done.2, s32[1]{0:T(128)} %bitcast.my_row, f32[1024,768]{1,0:T(8,128)S(1)} %copy-done), custom_call_target="tpu_custom_call" | custom-call | tf_op jit(solution)/shard_map/pick/pallas_call | solution.py:50
  10.8 6.4 %all-to-all-start = ((f32[8,32,768]{2,1,0:T(8,128)}), f32[8,32,768]{2,1,0:T(8,128)S(1)}, u32[]{:S(2)}, u32[]{:S(2)}) async-start(f32[8,32,768]{2,1,0:T(8,128)} %pick.1), calls=%async_computation | async-start | bytes 1572864 | tf_op jit(solution)/shard_map/all_to_all | solution.py:209
  17.9 0.9 %select_select_fusion.1 = f32[256,128]{1,0:T(8,128)S(1)} fusion(f32[256,128]{1,0:T(8,128)S(1)} %collective-permute-done, f32[256,128]{1,0:T(8,128)S(1)} %collective-permute-done.1, f32[256,128]{1,0:T(8,128)S(1)} %collective-permute-done.2, f32[1024,768]{1,0:T(8,128)} %matrix.3, pred[]{:T(512)S(6)} %eq.49, pred[]{:T(512)S(6)} %eq.48, pred[]{:T(512)S(6)} %eq.47), kind=kLoop, calls=%fused_computation.7 | loop fusion | flops 98304 | bytes 655363 | tf_op jit(solution)/shard_map/jit(_where)/select_n | solution.py:206
  18.9 0.7 collective-permute-start.8
  19.6 0.7 collective-permute-start.7
  20.2 0.7 collective-permute-start.6
  21.0 0.7 collective-permute-start.11
  21.7 0.7 collective-permute-start.10
  22.4 0.7 collective-permute-start.9
  23.1 2.4 %all-to-all-done = f32[8,32,768]{2,1,0:T(8,128)S(1)} async-done(((f32[8,32,768]{2,1,0:T(8,128)}), f32[8,32,768]{2,1,0:T(8,128)S(1)}, u32[]{:S(2)}, u32[]{:S(2)}) %all-to-all-start) | async-done | bytes 786464 | tf_op jit(solution)/shard_map/all_to_all | solution.py:209
  25.6 0.9 %broadcast_in_dim.2 = f32[8,32,768]{2,1,0:T(8,128)} broadcast(f32[32,768]{1,0:T(8,128)S(1)} %reduce_sum.9), dimensions={1,2} | broadcast | bytes 884736 | tf_op jit(solution)/shard_map/broadcast_in_dim | solution.py:212
  26.5 3.5 %all-to-all-start.1 = ((f32[8,32,768]{2,1,0:T(8,128)}), f32[8,32,768]{2,1,0:T(8,128)S(1)}, u32[]{:S(2)}, u32[]{:S(2)}) async-start(f32[8,32,768]{2,1,0:T(8,128)} %broadcast_in_dim.2), calls=%async_computation.1 | async-start | bytes 1572864 | tf_op jit(solution)/shard_map/all_to_all | solution.py:211
  30.1 1.3 %collective-permute-start.12 = (f32[1152,128]{1,0:T(8,128)S(1)}, f32[1152,128]{1,0:T(8,128)S(1)}, u32[]{:S(2)}, u32[]{:S(2)}) collective-permute-start(f32[1152,128]{1,0:T(8,128)S(1)} %fusion.2), channel_id=1, source_target_pairs={{0,1},{8,9},{16,17},{24,25},{2,3},{10,11},{18,19},{26,27},{4,5},{1... | collective-permute-start | bytes 1769480 | tf_op jit(solution)/shard_map/ppermute | solution.py:239
  31.5 33.7 %collective-permute-done.12 = f32[1152,128]{1,0:T(8,128)S(1)} collective-permute-done((f32[1152,128]{1,0:T(8,128)S(1)}, f32[1152,128]{1,0:T(8,128)S(1)}, u32[]{:S(2)}, u32[]{:S(2)}) %collective-permute-start.12) | collective-permute-done | bytes 589856 | tf_op jit(solution)/shard_map/ppermute | solution.py:239
  65.9 4.1 %invert.1.inverse = f32[128,128]{1,0:T(8,128)} custom-call(f32[128,128]{1,0:T(8,128)} %slice.69.block), custom_call_target="tpu_custom_call" | custom-call | tf_op jit(solution)/shard_map/invert/pallas_call | solution.py:89
  70.0 0.8 %copy-done.1 = f32[128,128]{1,0:T(8,128)S(1)} copy-done((f32[128,128]{1,0:T(8,128)S(1)}, f32[128,128]{1,0:T(8,128)}, u32[]{:S(2)}) %copy-start.1) | copy-done | bytes 65560
  70.9 4.4 %solve.1 = (f32[1024,768]{1,0:T(8,128)S(1)}, f32[128,768]{1,0:T(8,128)S(1)}) custom-call(s32[128]{0:T(128)S(1)} %copy-done.3, s32[1]{0:T(128)} %bitcast.my_row, f32[1024,768]{1,0:T(8,128)} %matrix.3, f32[128,128]{1,0:T(8,128)S(1)} %copy-done.1, f32[8,32,768]{2,1,0:T(8,128)S(1)} %all-to-all-done.1.rows), custom_call_target="tpu_custom_call" | custom-call | tf_op jit(solution)/shard_map/solve/pallas_call | solution.py:119
  75.3 4.7 %update.1 = f32[1024,768]{1,0:T(8,128)} custom-call(s32[3]{0:T(128)S(1)} %pad_add_fusion.place, f32[4,256,128]{2,1,0:T(8,128)S(1)} %bitcast.4, f32[128,768]{1,0:T(8,128)S(1)} %get-tuple-element.7.solved, f32[1024,768]{1,0:T(8,128)S(1)} %get-tuple-element.8.swapped), custom_call_target="tpu_custom_call" | custom-call | tf_op jit(solution)/shard_map/update/pallas_call | solution.py:160
  (37 shorter events, 4.3 us)
Async XLA Ops:
  0.8 0.7 collective-permute-start.3
  2.4 14.8 %collective-permute-start.4 = (f32[128,128]{1,0:T(8,128)S(1)}, f32[128,128]{1,0:T(8,128)S(1)}, u32[]{:S(2)}, u32[]{:S(2)}) collective-permute-start(f32[128,128]{1,0:T(8,128)S(1)} %broadcast_select_fusion.1), channel_id=1, source_target_pairs={{0,32},{128,160}} | collective-permute-start | bytes 196616 | tf_op jit(solution)/shard_map/ppermute | solution.py:196
  4.1 13.7 %collective-permute-start.2 = (f32[256,128]{1,0:T(8,128)S(1)}, f32[256,128]{1,0:T(8,128)S(1)}, u32[]{:S(2)}, u32[]{:S(2)}) collective-permute-start(f32[256,128]{1,0:T(8,128)S(1)} %get-tuple-element.9), channel_id=1, source_target_pairs={{0,2},{32,34},{64,66},{96,98},{128,130},{160,162},{192,194},{224,2... | collective-permute-start | bytes 393224 | tf_op jit(solution)/shard_map/ppermute | solution.py:205
  4.8 13.1 %collective-permute-start.1 = (f32[256,128]{1,0:T(8,128)S(1)}, f32[256,128]{1,0:T(8,128)S(1)}, u32[]{:S(2)}, u32[]{:S(2)}) collective-permute-start(f32[256,128]{1,0:T(8,128)S(1)} %get-tuple-element.10), channel_id=1, source_target_pairs={{0,4},{32,36},{64,68},{96,100},{128,132},{160,164},{192,196},{224,... | collective-permute-start | bytes 393224 | tf_op jit(solution)/shard_map/ppermute | solution.py:205
  5.5 12.4 %collective-permute-start = (f32[256,128]{1,0:T(8,128)S(1)}, f32[256,128]{1,0:T(8,128)S(1)}, u32[]{:S(2)}, u32[]{:S(2)}) collective-permute-start(f32[256,128]{1,0:T(8,128)S(1)} %get-tuple-element.11), channel_id=1, source_target_pairs={{0,6},{32,38},{64,70},{96,102},{128,134},{160,166},{192,198},{224,... | collective-permute-start | bytes 393224 | tf_op jit(solution)/shard_map/ppermute | solution.py:205
  6.1 1.9 %copy-start = (f32[1024,768]{1,0:T(8,128)S(1)}, f32[1024,768]{1,0:T(8,128)}, u32[]{:S(2)}) copy-start(f32[1024,768]{1,0:T(8,128)} %matrix.3) | copy-start | bytes 9437188
  8.0 0.7 copy-start.2
  10.8 14.7 %all-to-all-start = ((f32[8,32,768]{2,1,0:T(8,128)}), f32[8,32,768]{2,1,0:T(8,128)S(1)}, u32[]{:S(2)}, u32[]{:S(2)}) async-start(f32[8,32,768]{2,1,0:T(8,128)} %pick.1), calls=%async_computation | async-start | bytes 1572864 | tf_op jit(solution)/shard_map/all_to_all | solution.py:209
  17.2 1.6 %collective-permute-start.5 = (f32[128,128]{1,0:T(8,128)S(1)}, f32[128,128]{1,0:T(8,128)S(1)}, u32[]{:S(2)}, u32[]{:S(2)}) collective-permute-start(f32[128,128]{1,0:T(8,128)S(1)} %broadcast_select_fusion.2), channel_id=1, source_target_pairs={{0,96},{32,64},{128,224},{160,192}} | collective-permute-start | bytes 196616 | tf_op jit(solution)/shard_map/ppermute | solution.py:196
  18.9 2.1 %collective-permute-start.8 = (f32[384,128]{1,0:T(8,128)S(1)}, f32[384,128]{1,0:T(8,128)S(1)}, u32[]{:S(2)}, u32[]{:S(2)}) collective-permute-start(f32[384,128]{1,0:T(8,128)S(1)} %pad_maximum_fusion), channel_id=1, source_target_pairs={{0,8},{2,10},{4,12},{6,14},{32,40},{34,42},{36,44},{38,46},{64,72}... | collective-permute-start | bytes 589832 | tf_op jit(solution)/shard_map/ppermute | solution.py:218
  19.6 1.4 %collective-permute-start.7 = (f32[384,128]{1,0:T(8,128)S(1)}, f32[384,128]{1,0:T(8,128)S(1)}, u32[]{:S(2)}, u32[]{:S(2)}) collective-permute-start(f32[384,128]{1,0:T(8,128)S(1)} %pad_maximum_fusion), channel_id=1, source_target_pairs={{0,16},{2,18},{4,20},{6,22},{32,48},{34,50},{36,52},{38,54},{64,80... | collective-permute-start | bytes 589832 | tf_op jit(solution)/shard_map/ppermute | solution.py:218
  20.2 0.7 collective-permute-start.6
  21.0 9.0 %collective-permute-start.11 = (f32[384,128]{1,0:T(8,128)S(1)}, f32[384,128]{1,0:T(8,128)S(1)}, u32[]{:S(2)}, u32[]{:S(2)}) collective-permute-start(f32[384,128]{1,0:T(8,128)S(1)} %select_select_fusion), channel_id=1, source_target_pairs={{0,6},{8,14},{16,22},{24,30},{2,0},{10,8},{18,16},{26,24},{4,2},{1... | collective-permute-start | bytes 589832 | tf_op jit(solution)/shard_map/ppermute | solution.py:226
  21.7 1.4 %collective-permute-start.10 = (f32[384,128]{1,0:T(8,128)S(1)}, f32[384,128]{1,0:T(8,128)S(1)}, u32[]{:S(2)}, u32[]{:S(2)}) collective-permute-start(f32[384,128]{1,0:T(8,128)S(1)} %select_select_fusion), channel_id=1, source_target_pairs={{0,4},{8,12},{16,20},{24,28},{2,6},{10,14},{18,22},{26,30},{4,0},{... | collective-permute-start | bytes 589832 | tf_op jit(solution)/shard_map/ppermute | solution.py:226
  22.4 0.7 collective-permute-start.9
  25.5 44.5 %copy-start.3 = (s32[128]{0:T(128)S(1)}, s32[128]{0:T(128)}, u32[]{:S(2)}) copy-start(s32[128]{0:T(128)} %pivots.3) | copy-start | bytes 1540
  26.5 43.5 %all-to-all-start.1 = ((f32[8,32,768]{2,1,0:T(8,128)}), f32[8,32,768]{2,1,0:T(8,128)S(1)}, u32[]{:S(2)}, u32[]{:S(2)}) async-start(f32[8,32,768]{2,1,0:T(8,128)} %broadcast_in_dim.2), calls=%async_computation.1 | async-start | bytes 1572864 | tf_op jit(solution)/shard_map/all_to_all | solution.py:211
  30.1 35.1 %collective-permute-start.12 = (f32[1152,128]{1,0:T(8,128)S(1)}, f32[1152,128]{1,0:T(8,128)S(1)}, u32[]{:S(2)}, u32[]{:S(2)}) collective-permute-start(f32[1152,128]{1,0:T(8,128)S(1)} %fusion.2), channel_id=1, source_target_pairs={{0,1},{8,9},{16,17},{24,25},{2,3},{10,11},{18,19},{26,27},{4,5},{1... | collective-permute-start | bytes 1769480 | tf_op jit(solution)/shard_map/ppermute | solution.py:239
  70.0 0.8 %copy-start.1 = (f32[128,128]{1,0:T(8,128)S(1)}, f32[128,128]{1,0:T(8,128)}, u32[]{:S(2)}) copy-start(f32[128,128]{1,0:T(8,128)} %invert.1.inverse) | copy-start | bytes 196612

commit v2 on v0

v2 whole, which is shorter than its diff:
```python
import functools

import jax
import jax.numpy as jnp
from jax import lax
from jax.experimental import pallas as pl
from jax.experimental.pallas import tpu as pltpu
from jax.sharding import Mesh, PartitionSpec as P

NB = 128
EXACT = lax.Precision.HIGHEST
ROWS = ("zl", "y")
COLS = ("zh", "x", "c")
N_Y, N_X, N_ZH, N_C = 4, 4, 4, 2
N_PROW, N_PCOL = 8, 32
N_PART = 4
STEP = NB // N_PROW
SLOTS = 32
BLOCK = 16
PLAN_ROWS = 8

VMEM = pl.BlockSpec(memory_space=pltpu.VMEM)
SMEM = pl.BlockSpec(memory_space=pltpu.SMEM)
ANY = pl.BlockSpec(memory_space=pl.ANY)


SMALL = pltpu.CompilerParams(vmem_limit_bytes=12 << 20)
LARGE = pltpu.CompilerParams(vmem_limit_bytes=56 << 20)


def prow_id(zl, y):
    return zl * N_Y + y


def pcol_id(zh, x, c):
    return (zh * N_X + x) * N_C + c


def my_place():
    row = prow_id(lax.axis_index("zl"), lax.axis_index("y"))
    col = pcol_id(*(lax.axis_index(name) for name in COLS))
    return row, col


NEAR = (1, 0, 3, 2)
FAR = (3, 2, 1, 0)


def send_cols(value, pairs):
    return lax.ppermute(value, COLS, [(pcol_id(*s), pcol_id(*t)) for s, t in pairs])


def send_rows(value, pairs, cols=range(N_PCOL)):
    pairs = [(prow_id(*s) * N_PCOL + q, prow_id(*t) * N_PCOL + q) for s, t in pairs for q in cols]
    return lax.ppermute(value, ROWS + COLS, pairs)


def after(value, first):
    return lax.optimization_barrier((value, first))[0]


def owned_row(pivot, my_row):
    is_owned = ((pivot >> 7) & (N_PROW - 1)) == my_row
    return is_owned, jnp.where(is_owned, ((pivot >> 10) << 7) + (pivot & (NB - 1)), 0)


def to_column(row):
    size = row.shape[1]
    rows = lax.broadcasted_iota(jnp.int32, (size, size), 0)
    cols = lax.broadcasted_iota(jnp.int32, (size, size), 1)
    return jnp.sum(jnp.where(rows == cols, row, 0.0), axis=1, keepdims=True)


def ranks_of(pivots):
    owner = ((pivots >> 7) & (N_PROW - 1)).astype(jnp.float32)
    rows = lax.broadcasted_iota(jnp.int32, (NB, NB), 0)
    cols = lax.broadcasted_iota(jnp.int32, (NB, NB), 1)
    before = (to_column(owner) == owner) & (rows < cols)
    return jnp.sum(jnp.where(before, 1.0, 0.0), axis=0, keepdims=True)


def plan_kernel(pivots, out):
    my_row, _ = my_place()
    ranks = ranks_of(pivots[...])
    owner = (pivots[...] >> 7) & (N_PROW - 1)
    is_owned, row = owned_row(pivots[...], my_row)
    rank = to_column(jnp.where(is_owned, ranks, -1.0))
    wanted = lax.broadcasted_iota(jnp.int32, (NB, NB), 1).astype(jnp.float32)
    rows = jnp.where(rank == wanted, to_column(row.astype(jnp.float32)), 0.0)
    count = jnp.sum(is_owned.astype(jnp.float32), axis=1, keepdims=True)
    most = jnp.max(ranks, axis=1, keepdims=True) + 1.0
    out[...] = jnp.zeros_like(out)
    out[0:1, :] = owner * NB + ranks.astype(jnp.int32)
    out[1:2, :] = jnp.sum(rows, axis=0, keepdims=True).astype(jnp.int32)
    out[2:3, :] = jnp.broadcast_to(count, (1, NB)).astype(jnp.int32)
    out[3:4, :] = jnp.broadcast_to(most, (1, NB)).astype(jnp.int32)


def make_plan(pivots):
    return pl.pallas_call(
        plan_kernel,
        out_shape=jax.ShapeDtypeStruct((PLAN_ROWS, NB), jnp.int32),
        in_specs=[VMEM],
        out_specs=VMEM,
        compiler_params=SMALL,
        cost_estimate=pl.CostEstimate(flops=0, bytes_accessed=3 << 20, transcendentals=0),
        name="plan",
    )(pivots)


def pack_kernel(turn, plan_hbm, matrix, out, plan, held, top, moved, sems, row_sems, out_sems):
    my_row, _ = my_place()
    on_top = my_row == 0
    load = pltpu.make_async_copy(plan_hbm, plan, sems.at[0])
    load_top = pltpu.make_async_copy(matrix.at[pl.ds(0, NB), :], top, sems.at[1])
    load.start()

    @pl.when(on_top)
    def _():
        load_top.start()

    load.wait()
    first = turn[0] * SLOTS
    copies = [
        pltpu.make_async_copy(
            matrix.at[pl.ds(plan[1, first + i], 1), :], held.at[pl.ds(i, 1), :], row_sems.at[i]
        )
        for i in range(SLOTS)
    ]
    for copy in copies:
        copy.start()

    def held_copy(j):
        return pltpu.make_async_copy(held, out.at[j, pl.ds(0, SLOTS), :], out_sems.at[j])

    def moved_copy(j):
        return pltpu.make_async_copy(
            moved.at[pl.ds(j * SLOTS, SLOTS), :],
            out.at[j, pl.ds(SLOTS, SLOTS), :],
            out_sems.at[N_PROW + j],
        )

    @pl.when(on_top)
    def _():
        load_top.wait()

        def move(j, _):
            for i in range(8):
                entry = plan[0, j * 8 + i]
                rank = entry & (NB - 1)
                place = ((entry >> 7) << 5) + (rank & (SLOTS - 1))
                place = jnp.where((rank >> 5) == turn[0], place, N_PROW * SLOTS)
                moved[pl.ds(place, 1), :] = top[pl.ds(j * 8 + i, 1), :]
            return 0

        lax.fori_loop(0, NB // 8, move, 0)
        for j in range(N_PROW):
            moved_copy(j).start()

    for copy in copies:
        copy.wait()
    for j in range(N_PROW):
        held_copy(j).start()

    @pl.when(on_top)
    def _():
        for j in range(N_PROW):
            moved_copy(j).wait()

    for j in range(N_PROW):
        held_copy(j).wait()


def pack(turn, plan, matrix):
    cols = matrix.shape[1]
    return pl.pallas_call(
        pack_kernel,
        out_shape=jax.ShapeDtypeStruct((N_PROW, 2 * SLOTS, cols), jnp.float32),
        in_specs=[SMEM, ANY, ANY],
        out_specs=ANY,
        scratch_shapes=[
            pltpu.SMEM((PLAN_ROWS, NB), jnp.int32),
            pltpu.VMEM((SLOTS, cols), jnp.float32),
            pltpu.VMEM((NB, cols), jnp.float32),
            pltpu.VMEM(((N_PROW + 1) * SLOTS, cols), jnp.float32),
            pltpu.SemaphoreType.DMA((2,)),
            pltpu.SemaphoreType.DMA((SLOTS,)),
            pltpu.SemaphoreType.DMA((2 * N_PROW,)),
        ],
        compiler_params=LARGE,
        cost_estimate=pl.CostEstimate(flops=0, bytes_accessed=6 << 20, transcendentals=0),
        name="pack",
    )(turn, plan, matrix)


def split(value):
    first = value.astype(jnp.bfloat16)
    rest = value - first.astype(jnp.float32)
    second = rest.astype(jnp.bfloat16)
    third = (rest - second.astype(jnp.float32)).astype(jnp.bfloat16)
    return first, second, third


def exact_dot(a, b):
    a1, a2, a3 = split(a)
    b1, b2, b3 = split(b)
    product = functools.partial(jnp.dot, preferred_element_type=jnp.float32)
    lead = jnp.concatenate([a1, a2], axis=1)
    total = product(jnp.concatenate([a1, a3], axis=1), jnp.concatenate([b3, b1], axis=0))
    total = total + product(lead, jnp.concatenate([b2, b2], axis=0))
    return total + product(lead, jnp.concatenate([b1, b1], axis=0))


def inverse_of(lower):
    rows = lax.broadcasted_iota(jnp.int32, (NB, NB), 0)
    cols = lax.broadcasted_iota(jnp.int32, (NB, NB), 1)
    block_bits = BLOCK.bit_length() - 1
    offset = cols - ((rows >> block_bits) << block_bits)
    lower = jnp.where(rows > cols, lower, 0.0)
    inverse = jnp.where(rows == cols, 1.0, 0.0).reshape(NB // BLOCK, BLOCK, NB)
    for j in range(BLOCK - 1):
        column = jnp.sum(jnp.where(offset == j, lower, 0.0), axis=1, keepdims=True)
        column = column.reshape(NB // BLOCK, BLOCK, 1)
        inverse = inverse - column * inverse[:, j : j + 1, :]
    inverse = inverse.reshape(NB, NB)
    size = BLOCK
    while size < NB:
        shift = size.bit_length()
        same = (rows >> shift) == (cols >> shift)
        below = ((rows & size) != 0) & ((cols & size) == 0)
        part = jnp.where(same & below, lower, 0.0)
        inverse = inverse - exact_dot(inverse, exact_dot(part, inverse))
        size *= 2
    return inverse


def weigh_kernel(block, panel_hbm, first, second, other, panel, sem):
    my_row, my_col = my_place()

    @pl.when(my_col == 0)
    def _():
        copy = pltpu.make_async_copy(panel_hbm, panel, sem)
        copy.start()
        inverse = inverse_of(block[...])
        copy.wait()
        start = 0
        for out in (first, second, other):
            out[...] = exact_dot(panel[start : start + out.shape[0], :], inverse)
            start += out.shape[0]

        @pl.when(my_row == 0)
        def _():
            first[:NB, :] = -inverse


def weigh(block, panel):
    height = panel.shape[0]
    quarter = jax.ShapeDtypeStruct((height // 4, NB), jnp.float32)
    half = jax.ShapeDtypeStruct((height // 2, NB), jnp.float32)
    return pl.pallas_call(
        weigh_kernel,
        out_shape=(quarter, quarter, half),
        in_specs=[VMEM, ANY],
        out_specs=(VMEM, VMEM, VMEM),
        scratch_shapes=[pltpu.VMEM((height, NB), jnp.float32), pltpu.SemaphoreType.DMA],
        compiler_params=SMALL,
        name="weigh",
    )(block, panel)


def prepare_kernel(plan_hbm, rows, rest, matrix, base, factors, picked, own, plan, sems):
    my_row, my_col = my_place()
    load = pltpu.make_async_copy(plan_hbm, plan, sems.at[0])
    whole = pltpu.make_async_copy(matrix, base, sems.at[1])
    load.start()
    whole.start()
    load.wait()

    def find(j, _):
        for i in range(8):
            k = j * 8 + i
            entry = plan[0, k]
            place = entry & (SLOTS - 1)
            picked[pl.ds(k, 1), :] = rows[entry >> 7, pl.ds(place, 1), :]
        return 0

    lax.fori_loop(0, NB // 8, find, 0)

    def fetch(turn, source, place, target):
        copy = pltpu.make_async_copy(
            rest.at[turn - 1, source, pl.ds(place, 1), :], target, sems.at[0]
        )
        copy.start()
        copy.wait()

    @pl.when(plan[3, 0] > SLOTS)
    def _():
        def find_late(k, _):
            entry = plan[0, k]
            rank = entry & (NB - 1)

            @pl.when(rank >= SLOTS)
            def _():
                fetch(rank >> 5, entry >> 7, rank & (SLOTS - 1), picked.at[pl.ds(k, 1), :])

            return 0

        lax.fori_loop(0, NB, find_late, 0)

    first, second, third = split(picked[...])
    factors[0, :NB, :] = first
    factors[0, NB:, :] = first
    factors[1, :NB, :] = second
    factors[1, NB:, :] = second
    factors[2, :NB, :] = third
    factors[2, NB:, :] = first
    whole.wait()

    @pl.when(my_col == 0)
    def _():
        own[...] = base[:, :NB]

    def swap(i, _):
        base[pl.ds(plan[1, i], 1), :] = rows[0, pl.ds(SLOTS + i, 1), :]
        return 0

    lax.fori_loop(0, jnp.minimum(plan[2, 0], SLOTS), swap, 0)

    def swap_late(i, _):
        place = SLOTS + (i & (SLOTS - 1))
        fetch(i >> 5, 0, place, base.at[pl.ds(plan[1, i], 1), :])
        return 0

    lax.fori_loop(SLOTS, jnp.maximum(plan[2, 0], SLOTS), swap_late, 0)

    @pl.when(my_row == 0)
    def _():
        base[:NB, :] = jnp.zeros((NB, base.shape[1]), jnp.float32)

    @pl.when(my_col == 0)
    def _():
        base[:, :NB] = own[...]
        factors[:, :, :NB] = jnp.zeros((3, 2 * NB, NB), jnp.bfloat16)


def prepare(plan, rows, rest, matrix):
    height, cols = matrix.shape
    return pl.pallas_call(
        prepare_kernel,
        out_shape=(
            jax.ShapeDtypeStruct(matrix.shape, jnp.float32),
            jax.ShapeDtypeStruct((3, 2 * NB, cols), jnp.bfloat16),
        ),
        in_specs=[ANY, VMEM, ANY, ANY],
        out_specs=(VMEM, VMEM),
        scratch_shapes=[
            pltpu.VMEM((NB, cols), jnp.float32),
            pltpu.VMEM((height, NB), jnp.float32),
            pltpu.SMEM((PLAN_ROWS, NB), jnp.int32),
            pltpu.SemaphoreType.DMA((2,)),
        ],
        compiler_params=SMALL,
        cost_estimate=pl.CostEstimate(flops=0, bytes_accessed=9 << 20, transcendentals=0),
        name="prepare",
    )(plan, rows, rest, matrix)


def holdings():
    x, c = lax.axis_index("x"), lax.axis_index("c")
    bits = ((x == 1) | (x == 2)).astype(jnp.int32), (x >= 2).astype(jnp.int32)
    mine = jnp.where(c == 0, bits[0], bits[1])
    other = jnp.where(c == 0, bits[1], bits[0])
    return c, mine, other


def update_kernel(late, mine, theirs, factors, base, *refs):
    out, buffer, sems = refs[-3:]
    core, my_bit, other_bit = holdings()
    height = mine.shape[0]
    quarters = (2 * core + (my_bit ^ late), 2 * (1 - core) + (other_bit ^ late))
    copies = []
    for s, (piece, quarter) in enumerate(zip((mine, theirs), quarters)):
        start = pl.multiple_of(quarter * height, height)
        first, second, third = split(piece[...])
        lead = jnp.concatenate([first, second], axis=1)
        tail = jnp.concatenate([first, third], axis=1)
        product = functools.partial(jnp.dot, preferred_element_type=jnp.float32)
        total = product(tail, factors[2]) + product(lead, factors[1]) + product(lead, factors[0])
        buffer[s] = base[pl.ds(start, height), :] - total
        copy = pltpu.make_async_copy(buffer.at[s], out.at[pl.ds(start, height), :], sems.at[s])
        copy.start()
        copies.append(copy)
    for copy in copies:
        copy.wait()


def update(late, mine, theirs, factors, base, done):
    height, cols = mine.shape[0], base.shape[1]
    extra = [] if done is None else [done]
    return pl.pallas_call(
        functools.partial(update_kernel, late),
        out_shape=jax.ShapeDtypeStruct(base.shape, jnp.float32),
        in_specs=[VMEM] * 4 + [ANY] * len(extra),
        out_specs=ANY,
        scratch_shapes=[
            pltpu.VMEM((2, height, cols), jnp.float32),
            pltpu.SemaphoreType.DMA((2,)),
        ],
        input_output_aliases={4: 0} if extra else {},
        compiler_params=SMALL,
        cost_estimate=pl.CostEstimate(flops=0, bytes_accessed=4 << 20, transcendentals=0),
        name="update",
    )(mine, theirs, factors, base, *extra)


def blank_kernel(out):
    pass


def blank(shape):
    return pl.pallas_call(
        blank_kernel,
        out_shape=jax.ShapeDtypeStruct(shape, jnp.float32),
        out_specs=ANY,
        compiler_params=SMALL,
        name="blank",
    )()


def later_rounds(plan, matrix):
    most = plan[3, 0]

    def body(state):
        turn, rest = state
        sent = pack(turn.reshape(1), plan, matrix)
        got = lax.all_to_all(sent, ROWS, 0, 0)
        return turn + 1, lax.dynamic_update_slice(rest, got[None], (turn - 1, 0, 0, 0))

    rest = blank((NB // SLOTS - 1, N_PROW, 2 * SLOTS, matrix.shape[1]))
    return lax.while_loop(lambda state: state[0] * SLOTS < most, body, (jnp.int32(1), rest))[1]


def local(matrix, pivot_rows):
    zh, x, c = (lax.axis_index(name) for name in COLS)
    zl, y = (lax.axis_index(name) for name in ROWS)
    panel = lax.optimization_barrier(matrix[:, :NB])
    lower = panel[:NB]
    got = send_rows(lower, [((0, 0), (1, 0))])
    plan = make_plan(pivot_rows.reshape(1, NB))
    lower = jnp.where(zl == 1, after(got, plan), lower)
    got = send_rows(lower, [((a, 0), (a, 1)) for a in (0, 1)])
    sent = pack(jnp.zeros((1,), jnp.int32), after(plan, lower), matrix)
    lower = jnp.where(y == 1, after(got, sent), lower)
    got = send_rows(lower, [((a, s), (a, t)) for a in (0, 1) for s, t in ((0, 3), (1, 2))])
    lower = jnp.where(y >= 2, got, lower)
    rows = lax.all_to_all(after(sent, lower), ROWS, 0, 0)
    rest = later_rounds(after(plan, sent), matrix)
    first, second, half = weigh(lower, panel)

    zs, xs = range(N_ZH), range(N_X)
    quarter = matrix.shape[0] // N_PART
    got = send_cols(half, [((0, 0, 0), (0, 0, 1))])
    first = jnp.where(c == 0, first, got[:quarter])
    second = jnp.where(c == 0, second, got[quarter:])
    got = send_cols(second, [((0, 0, 0), (0, 1, 0)), ((0, 0, 1), (0, 3, 1))])
    piece = jnp.where(x == jnp.where(c == 0, 1, 3), got, first)
    got = send_cols(
        piece,
        [((0, s, 0), (0, t, 0)) for s, t in ((0, 3), (1, 2))]
        + [((0, s, 1), (0, t, 1)) for s, t in ((0, 1), (3, 2))],
    )
    piece = jnp.where((x == 2) | (x == jnp.where(c == 0, 3, 1)), got, piece)
    got = send_cols(
        piece,
        [((0, a, 0), (1, a, 0)) for a in xs] + [((0, a, 1), (3, a, 1)) for a in xs],
    )
    piece = jnp.where(zh == jnp.where(c == 0, 1, 3), got, piece)
    base, factors = prepare(plan, after(rows, piece), rest, matrix)
    got = send_cols(
        piece,
        [((s, a, 0), (t, a, 0)) for a in xs for s, t in ((0, 3), (1, 2))]
        + [((s, a, 1), (t, a, 1)) for a in xs for s, t in ((0, 1), (3, 2))],
    )
    got = after(got, factors)
    piece = jnp.where((zh == 2) | (zh == jnp.where(c == 0, 3, 1)), got, piece)
    chips = [(b, a) for a in xs for b in zs]
    other = send_cols(piece, [((b, a, d), (b, a, 1 - d)) for b, a in chips for d in (0, 1)])
    across = send_cols(
        piece,
        [((b, a, 0), (b, NEAR[a], 0)) for b, a in chips]
        + [((b, a, 1), (b, FAR[a], 1)) for b, a in chips],
    )
    crossed = send_cols(
        piece,
        [((b, a, 0), (b, NEAR[a], 1)) for b, a in chips]
        + [((b, a, 1), (b, FAR[a], 0)) for b, a in chips],
    )
    out = update(0, piece, other, factors, base, None)
    across, crossed, out = lax.optimization_barrier((across, crossed, out))
    return update(1, across, crossed, factors, base, out)


def solution(mesh):
    fine = Mesh(mesh.devices.reshape(2, N_Y, N_ZH, N_X, N_C), ROWS + COLS)
    placed = (P(ROWS, COLS), P())
    return jax.shard_map(
        local, mesh=fine, in_specs=placed, out_specs=P(ROWS, COLS), check_vma=False
    )
```

time: 413 us -> 57.4 us (0.14)
  the two profiles are of different devices: /device:TPU:1 before, /device:TPU:169 now
where the time goes in v2:
time: 57.4 us; the launch traced here: 56.9 us
  starting transfers between devices  23.5 us (41%)
  waiting for transfers between devices  20.7 us (36%)
  Pallas kernels  9.51 us (17%)
  local copies, waits for them, and re-layouts  2.24 us (4%)
    all_to_all x1, waiting for transfers between devices, local(): rows = lax.all_to_all(after(sent, lower), ROWS, 0, 0)  15.2 us
    ppermute x8, starting transfers between devices, send_cols(): lax.ppermute(value, COLS, [(pcol_id(*s), pcol_id(*t)) for s, t in pairs])  13.3 us
    all_to_all x1, starting transfers between devices, local(): rows = lax.all_to_all(after(sent, lower), ROWS, 0, 0)  6.86 us
    pallas_call x2, Pallas kernels, update(): pl.pallas_call(functools.partial(update_kernel, late), out_shape=jax.Shap...  3.86 us
    pallas_call x1, Pallas kernels, pack(): pl.pallas_call(pack_kernel, out_shape=jax.ShapeDtypeStruct((N_PROW, 2 * S...  3.44 us
    ppermute x3, starting transfers between devices, send_rows(): return lax.ppermute(value, ROWS + COLS, pairs)  3.25 us
    ppermute x3, waiting for transfers between devices, send_rows(): return lax.ppermute(value, ROWS + COLS, pairs)  3.09 us
    ppermute x8, waiting for transfers between devices, send_cols(): lax.ppermute(value, COLS, [(pcol_id(*s), pcol_id(*t)) for s, t in pairs])  2.39 us
  transfers between devices with their start and end apart: 12, of which 5 were waited for; matrix products, arithmetic and copies ran while one was open for 1% of the time, Pallas kernels for 13%

profile of v2, /device:TPU:169, one launch (start us, length us, event | category | flops | bytes accessed | tf_op | source)
XLA Modules:
  0.0 56.9 jit_solution(17232461036618872169)
XLA Ops:
  0.0 1.1 %slice.15.panel_hbm = f32[1024,128]{1,0:T(8,128)S(1)} slice(f32[1024,768]{1,0:T(8,128)} %matrix.3), slice={[0:1024], [0:128]} | slice | bytes 1048576 | tf_op jit(solution)/shard_map/slice | solution.py:446
  1.1 0.7 %collective-permute-start = (f32[128,128]{1,0:T(8,128)S(1)}, f32[128,128]{1,0:T(8,128)S(1)}, u32[]{:S(2)}, u32[]{:S(2)}) collective-permute-start(f32[128,128]{1,0:T(8,128)S(1)} %slice.20), channel_id=1, source_target_pairs={{0,128},{1,129},{2,130},{3,131},{4,132},{5,133},{6,134},{7,135},{8... | collective-permute-start | bytes 196616 | tf_op jit(solution)/shard_map/ppermute | solution.py:55
  1.8 0.6 %copy-done = s32[128]{0:T(128)S(1)} copy-done((s32[128]{0:T(128)S(1)}, s32[128]{0:T(128)}, u32[]{:S(2)}) %copy-start) | copy-done | bytes 536
  2.7 1.3 %collective-permute-start.1 = (f32[128,128]{1,0:T(8,128)S(1)}, f32[128,128]{1,0:T(8,128)S(1)}, u32[]{:S(2)}, u32[]{:S(2)}) collective-permute-start(f32[128,128]{1,0:T(8,128)S(1)} %broadcast_select_fusion.3), channel_id=1, source_target_pairs={{0,32},{1,33},{2,34},{3,35},{4,36},{5,37},{6,38},{7,39},{8,40},{9,... | collective-permute-start | bytes 196616 | tf_op jit(solution)/shard_map/ppermute | solution.py:55
  4.0 3.4 %pack.8 = f32[8,64,768]{2,1,0:T(8,128)} custom-call(s32[1]{0:T(128)} %constant.63.clone.1.turn, s32[8,128]{1,0:T(8,128)S(1)} %plan.1.plan_hbm, f32[1024,768]{1,0:T(8,128)} %matrix.3), custom_call_target="tpu_custom_call" | custom-call | bytes 6291456 | tf_op jit(solution)/shard_map/pack/pallas_call | solution.py:176
  7.4 1.8 %collective-permute-done.1 = f32[128,128]{1,0:T(8,128)S(1)} collective-permute-done((f32[128,128]{1,0:T(8,128)S(1)}, f32[128,128]{1,0:T(8,128)S(1)}, u32[]{:S(2)}, u32[]{:S(2)}) %collective-permute-start.1) | collective-permute-done | bytes 65568 | tf_op jit(solution)/shard_map/ppermute | solution.py:55
  9.2 1.3 %collective-permute-start.2 = (f32[128,128]{1,0:T(8,128)S(1)}, f32[128,128]{1,0:T(8,128)S(1)}, u32[]{:S(2)}, u32[]{:S(2)}) collective-permute-start(f32[128,128]{1,0:T(8,128)S(1)} %broadcast_select_fusion.4), channel_id=1, source_target_pairs={{0,96},{1,97},{2,98},{3,99},{4,100},{5,101},{6,102},{7,103},{8,104... | collective-permute-start | bytes 196616 | tf_op jit(solution)/shard_map/ppermute | solution.py:55
  10.5 1.3 %collective-permute-done.2 = f32[128,128]{1,0:T(8,128)S(1)} collective-permute-done((f32[128,128]{1,0:T(8,128)S(1)}, f32[128,128]{1,0:T(8,128)S(1)}, u32[]{:S(2)}, u32[]{:S(2)}) %collective-permute-start.2) | collective-permute-done | bytes 65568 | tf_op jit(solution)/shard_map/ppermute | solution.py:55
  11.9 6.9 %all-to-all-start.1 = ((f32[8,64,768]{2,1,0:T(8,128)}), f32[8,64,768]{2,1,0:T(8,128)S(1)}, u32[]{:S(2)}, u32[]{:S(2)}) async-start(f32[8,64,768]{2,1,0:T(8,128)} %pack.8), calls=%async_computation.1 | async-start | bytes 3145728 | tf_op jit(solution)/shard_map/all_to_all | solution.py:456
  18.7 0.7 %collective-permute-start.3 = (f32[512,128]{1,0:T(8,128)S(1)}, f32[512,128]{1,0:T(8,128)S(1)}, u32[]{:S(2)}, u32[]{:S(2)}) collective-permute-start(f32[512,128]{1,0:T(8,128)S(1)} %get-tuple-element.130), channel_id=1, source_target_pairs={{0,1},{32,33},{64,65},{96,97},{128,129},{160,161},{192,193},{224,2... | collective-permute-start | bytes 786440 | tf_op jit(solution)/shard_map/ppermute | solution.py:50
  19.5 0.7 %collective-permute-start.4 = (f32[256,128]{1,0:T(8,128)S(1)}, f32[256,128]{1,0:T(8,128)S(1)}, u32[]{:S(2)}, u32[]{:S(2)}) collective-permute-start(f32[256,128]{1,0:T(8,128)S(1)} %slice_select_fusion.1), channel_id=1, source_target_pairs={{0,2},{1,7},{32,34},{33,39},{64,66},{65,71},{96,98},{97,103},{128,... | collective-permute-start | bytes 393224 | tf_op jit(solution)/shard_map/ppermute | solution.py:50
  20.2 0.7 %collective-permute-start.5 = (f32[256,128]{1,0:T(8,128)S(1)}, f32[256,128]{1,0:T(8,128)S(1)}, u32[]{:S(2)}, u32[]{:S(2)}) collective-permute-start(f32[256,128]{1,0:T(8,128)S(1)} %fusion), channel_id=1, source_target_pairs={{0,6},{2,4},{1,3},{7,5},{32,38},{34,36},{33,35},{39,37},{64,70},{6... | collective-permute-start | bytes 393224 | tf_op jit(solution)/shard_map/ppermute | solution.py:50
  20.9 0.7 %collective-permute-start.6 = (f32[256,128]{1,0:T(8,128)S(1)}, f32[256,128]{1,0:T(8,128)S(1)}, u32[]{:S(2)}, u32[]{:S(2)}) collective-permute-start(f32[256,128]{1,0:T(8,128)S(1)} %broadcast_select_fusion), channel_id=1, source_target_pairs={{0,8},{2,10},{4,12},{6,14},{1,25},{3,27},{5,29},{7,31},{32,40},{34... | collective-permute-start | bytes 393224 | tf_op jit(solution)/shard_map/ppermute | solution.py:50
  22.1 1.3 %collective-permute-start.7 = (f32[256,128]{1,0:T(8,128)S(1)}, f32[256,128]{1,0:T(8,128)S(1)}, u32[]{:S(2)}, u32[]{:S(2)}) collective-permute-start(f32[256,128]{1,0:T(8,128)S(1)} %broadcast_select_fusion.1), channel_id=1, source_target_pairs={{0,24},{8,16},{2,26},{10,18},{4,28},{12,20},{6,30},{14,22},{1,9},{... | collective-permute-start | bytes 393224 | tf_op jit(solution)/shard_map/ppermute | solution.py:50
  23.4 15.2 %all-to-all-done.1.rows = f32[8,64,768]{2,1,0:T(8,128)S(1)} async-done(((f32[8,64,768]{2,1,0:T(8,128)}), f32[8,64,768]{2,1,0:T(8,128)S(1)}, u32[]{:S(2)}, u32[]{:S(2)}) %all-to-all-start.1) | async-done | bytes 1572896 | tf_op jit(solution)/shard_map/all_to_all | solution.py:456
  38.7 0.6 %while.14 = (s32[]{:T(128)}, f32[3,8,64,768]{3,2,1,0:T(8,128)}, s32[]{:T(128)}, s32[8,128]{1,0:T(8,128)S(1)}, f32[1024,768]{1,0:T(8,128)}, /*index=5*/s32[]{:T(128)}, s32[]{:T(128)}, s32[]{:T(128)}, s32[]{:T(128)}) while((s32[]{:T(128)}, f32[3,8,64,768]{3,2,1,0:T(8,128)}, s32[]{:T(128)}, s32[8,128]{1,0:T(8,128)S(1)}, f32[1024,768]{1,0:T(8,128)}, ...), condition=%wide.region_1.2_spmd, body=%wide.region_0.1_spmd.sunk | while | flops 7 | bytes 14155963 | solution.py:440
  39.2 2.0 %prepare.1 = (f32[1024,768]{1,0:T(8,128)S(1)}, bf16[3,256,768]{2,1,0:T(8,128)(2,1)S(1)}) custom-call(s32[8,128]{1,0:T(8,128)S(1)} %get-tuple-element.231, f32[8,64,768]{2,1,0:T(8,128)S(1)} %all-to-all-done.1.rows, f32[3,8,64,768]{3,2,1,0:T(8,128)} %get-tuple-element.135.rest, f32[1024,768]{1,0:T(8,128)} %get-tuple-element.219), custom_call_target="tpu_custom_call" | custom-call | bytes 9437184 | tf_op jit(solution)/shard_map/prepare/pallas_call | solution.py:348
  41.2 0.9 %collective-permute-done.7 = f32[256,128]{1,0:T(8,128)S(1)} collective-permute-done((f32[256,128]{1,0:T(8,128)S(1)}, f32[256,128]{1,0:T(8,128)S(1)}, u32[]{:S(2)}, u32[]{:S(2)}) %collective-permute-start.7) | collective-permute-done | bytes 131104 | tf_op jit(solution)/shard_map/ppermute | solution.py:50
  42.2 4.3 %collective-permute-start.10 = (f32[256,128]{1,0:T(8,128)S(1)}, f32[256,128]{1,0:T(8,128)S(1)}, u32[]{:S(2)}, u32[]{:S(2)}) collective-permute-start(f32[256,128]{1,0:T(8,128)S(1)} %broadcast_select_fusion.2.mine), channel_id=1, source_target_pairs={{0,1},{1,0},{8,9},{9,8},{16,17},{17,16},{24,25},{25,24},{2,3},{3,2... | collective-permute-start | bytes 393224 | tf_op jit(solution)/shard_map/ppermute | solution.py:50
  46.5 4.0 %collective-permute-start.8 = (f32[256,128]{1,0:T(8,128)S(1)}, f32[256,128]{1,0:T(8,128)S(1)}, u32[]{:S(2)}, u32[]{:S(2)}) collective-permute-start(f32[256,128]{1,0:T(8,128)S(1)} %broadcast_select_fusion.2.mine), channel_id=1, source_target_pairs={{0,2},{8,10},{16,18},{24,26},{2,0},{10,8},{18,16},{26,24},{4,6},{1... | collective-permute-start | bytes 393224 | tf_op jit(solution)/shard_map/ppermute | solution.py:50
  50.6 1.0 %collective-permute-start.9 = (f32[256,128]{1,0:T(8,128)S(1)}, f32[256,128]{1,0:T(8,128)S(1)}, u32[]{:S(2)}, u32[]{:S(2)}) collective-permute-start(f32[256,128]{1,0:T(8,128)S(1)} %broadcast_select_fusion.2.mine), channel_id=1, source_target_pairs={{0,3},{8,11},{16,19},{24,27},{2,1},{10,9},{18,17},{26,25},{4,7},{1... | collective-permute-start | bytes 393224 | tf_op jit(solution)/shard_map/ppermute | solution.py:50
  51.6 1.9 %update.2.refs_0_ = f32[1024,768]{1,0:T(8,128)} custom-call(f32[256,128]{1,0:T(8,128)S(1)} %broadcast_select_fusion.2.mine, f32[256,128]{1,0:T(8,128)S(1)} %collective-permute-done.10.theirs, bf16[3,256,768]{2,1,0:T(8,128)(2,1)S(1)} %get-tuple-element.136.factors, f32[1024,768]{1,0:T(8,128)S(1)} %get-tuple-element.138.base), custom_call_target="tpu_custom_call" | custom-call | bytes 4194304 | tf_op jit(solution)/shard_map/update/pallas_call | solution.py:400
  53.5 1.4 %collective-permute-done.9.theirs = f32[256,128]{1,0:T(8,128)S(1)} collective-permute-done((f32[256,128]{1,0:T(8,128)S(1)}, f32[256,128]{1,0:T(8,128)S(1)}, u32[]{:S(2)}, u32[]{:S(2)}) %collective-permute-start.9) | collective-permute-done | bytes 131104 | tf_op jit(solution)/shard_map/ppermute | solution.py:50
  55.0 1.9 %update.3 = f32[1024,768]{1,0:T(8,128)} custom-call(f32[256,128]{1,0:T(8,128)S(1)} %collective-permute-done.8.mine, f32[256,128]{1,0:T(8,128)S(1)} %collective-permute-done.9.theirs, bf16[3,256,768]{2,1,0:T(8,128)(2,1)S(1)} %get-tuple-element.136.factors, f32[1024,768]{1,0:T(8,128)S(1)} %get-tuple-element.138.base, ...), custom_call_target="tpu_custom_call", output_to_operand_aliasing={{}: (4, {})} | custom-call | bytes 4194304 | tf_op jit(solution)/shard_map/update/pallas_call | solution.py:400
  (21 shorter events, 0.9 us)
Async XLA Ops:
  1.1 1.6 %collective-permute-start = (f32[128,128]{1,0:T(8,128)S(1)}, f32[128,128]{1,0:T(8,128)S(1)}, u32[]{:S(2)}, u32[]{:S(2)}) collective-permute-start(f32[128,128]{1,0:T(8,128)S(1)} %slice.20), channel_id=1, source_target_pairs={{0,128},{1,129},{2,130},{3,131},{4,132},{5,133},{6,134},{7,135},{8... | collective-permute-start | bytes 196616 | tf_op jit(solution)/shard_map/ppermute | solution.py:55
  1.8 0.7 %copy-start = (s32[128]{0:T(128)S(1)}, s32[128]{0:T(128)}, u32[]{:S(2)}) copy-start(s32[128]{0:T(128)} %param.5) | copy-start | bytes 1540
  2.7 6.5 %collective-permute-start.1 = (f32[128,128]{1,0:T(8,128)S(1)}, f32[128,128]{1,0:T(8,128)S(1)}, u32[]{:S(2)}, u32[]{:S(2)}) collective-permute-start(f32[128,128]{1,0:T(8,128)S(1)} %broadcast_select_fusion.3), channel_id=1, source_target_pairs={{0,32},{1,33},{2,34},{3,35},{4,36},{5,37},{6,38},{7,39},{8,40},{9,... | collective-permute-start | bytes 196616 | tf_op jit(solution)/shard_map/ppermute | solution.py:55
  9.2 2.6 %collective-permute-start.2 = (f32[128,128]{1,0:T(8,128)S(1)}, f32[128,128]{1,0:T(8,128)S(1)}, u32[]{:S(2)}, u32[]{:S(2)}) collective-permute-start(f32[128,128]{1,0:T(8,128)S(1)} %broadcast_select_fusion.4), channel_id=1, source_target_pairs={{0,96},{1,97},{2,98},{3,99},{4,100},{5,101},{6,102},{7,103},{8,104... | collective-permute-start | bytes 196616 | tf_op jit(solution)/shard_map/ppermute | solution.py:55
  11.9 26.8 %all-to-all-start.1 = ((f32[8,64,768]{2,1,0:T(8,128)}), f32[8,64,768]{2,1,0:T(8,128)S(1)}, u32[]{:S(2)}, u32[]{:S(2)}) async-start(f32[8,64,768]{2,1,0:T(8,128)} %pack.8), calls=%async_computation.1 | async-start | bytes 3145728 | tf_op jit(solution)/shard_map/all_to_all | solution.py:456
  18.7 0.7 %collective-permute-start.3 = (f32[512,128]{1,0:T(8,128)S(1)}, f32[512,128]{1,0:T(8,128)S(1)}, u32[]{:S(2)}, u32[]{:S(2)}) collective-permute-start(f32[512,128]{1,0:T(8,128)S(1)} %get-tuple-element.130), channel_id=1, source_target_pairs={{0,1},{32,33},{64,65},{96,97},{128,129},{160,161},{192,193},{224,2... | collective-permute-start | bytes 786440 | tf_op jit(solution)/shard_map/ppermute | solution.py:50
  19.5 0.7 %collective-permute-start.4 = (f32[256,128]{1,0:T(8,128)S(1)}, f32[256,128]{1,0:T(8,128)S(1)}, u32[]{:S(2)}, u32[]{:S(2)}) collective-permute-start(f32[256,128]{1,0:T(8,128)S(1)} %slice_select_fusion.1), channel_id=1, source_target_pairs={{0,2},{1,7},{32,34},{33,39},{64,66},{65,71},{96,98},{97,103},{128,... | collective-permute-start | bytes 393224 | tf_op jit(solution)/shard_map/ppermute | solution.py:50
  20.2 0.7 %collective-permute-start.5 = (f32[256,128]{1,0:T(8,128)S(1)}, f32[256,128]{1,0:T(8,128)S(1)}, u32[]{:S(2)}, u32[]{:S(2)}) collective-permute-start(f32[256,128]{1,0:T(8,128)S(1)} %fusion), channel_id=1, source_target_pairs={{0,6},{2,4},{1,3},{7,5},{32,38},{34,36},{33,35},{39,37},{64,70},{6... | collective-permute-start | bytes 393224 | tf_op jit(solution)/shard_map/ppermute | solution.py:50
  20.9 1.2 %collective-permute-start.6 = (f32[256,128]{1,0:T(8,128)S(1)}, f32[256,128]{1,0:T(8,128)S(1)}, u32[]{:S(2)}, u32[]{:S(2)}) collective-permute-start(f32[256,128]{1,0:T(8,128)S(1)} %broadcast_select_fusion), channel_id=1, source_target_pairs={{0,8},{2,10},{4,12},{6,14},{1,25},{3,27},{5,29},{7,31},{32,40},{34... | collective-permute-start | bytes 393224 | tf_op jit(solution)/shard_map/ppermute | solution.py:50
  22.1 20.0 %collective-permute-start.7 = (f32[256,128]{1,0:T(8,128)S(1)}, f32[256,128]{1,0:T(8,128)S(1)}, u32[]{:S(2)}, u32[]{:S(2)}) collective-permute-start(f32[256,128]{1,0:T(8,128)S(1)} %broadcast_select_fusion.1), channel_id=1, source_target_pairs={{0,24},{8,16},{2,26},{10,18},{4,28},{12,20},{6,30},{14,22},{1,9},{... | collective-permute-start | bytes 393224 | tf_op jit(solution)/shard_map/ppermute | solution.py:50
  42.2 9.4 %collective-permute-start.10 = (f32[256,128]{1,0:T(8,128)S(1)}, f32[256,128]{1,0:T(8,128)S(1)}, u32[]{:S(2)}, u32[]{:S(2)}) collective-permute-start(f32[256,128]{1,0:T(8,128)S(1)} %broadcast_select_fusion.2.mine), channel_id=1, source_target_pairs={{0,1},{1,0},{8,9},{9,8},{16,17},{17,16},{24,25},{25,24},{2,3},{3,2... | collective-permute-start | bytes 393224 | tf_op jit(solution)/shard_map/ppermute | solution.py:50
  46.5 7.0 %collective-permute-start.8 = (f32[256,128]{1,0:T(8,128)S(1)}, f32[256,128]{1,0:T(8,128)S(1)}, u32[]{:S(2)}, u32[]{:S(2)}) collective-permute-start(f32[256,128]{1,0:T(8,128)S(1)} %broadcast_select_fusion.2.mine), channel_id=1, source_target_pairs={{0,2},{8,10},{16,18},{24,26},{2,0},{10,8},{18,16},{26,24},{4,6},{1... | collective-permute-start | bytes 393224 | tf_op jit(solution)/shard_map/ppermute | solution.py:50
  50.6 4.4 %collective-permute-start.9 = (f32[256,128]{1,0:T(8,128)S(1)}, f32[256,128]{1,0:T(8,128)S(1)}, u32[]{:S(2)}, u32[]{:S(2)}) collective-permute-start(f32[256,128]{1,0:T(8,128)S(1)} %broadcast_select_fusion.2.mine), channel_id=1, source_target_pairs={{0,3},{8,11},{16,19},{24,27},{2,1},{10,9},{18,17},{26,25},{4,7},{1... | collective-permute-start | bytes 393224 | tf_op jit(solution)/shard_map/ppermute | solution.py:50

commit v3 on v2

--- a/solution.py
+++ b/solution.py
@@ -234,7 +234,8 @@
     return inverse
 
 
-def weigh_kernel(block, panel_hbm, first, second, other, panel, sem):
+def weigh_kernel(block, panel_hbm, *refs):
+    quarters, (panel, sem) = refs[:N_PART], refs[N_PART:]
     my_row, my_col = my_place()
 
     @pl.when(my_col == 0)
@@ -243,25 +244,23 @@
         copy.start()
         inverse = inverse_of(block[...])
         copy.wait()
-        start = 0
-        for out in (first, second, other):
-            out[...] = exact_dot(panel[start : start + out.shape[0], :], inverse)
-            start += out.shape[0]
+        height = quarters[0].shape[0]
+        for q, out in enumerate(quarters):
+            out[...] = exact_dot(panel[q * height : (q + 1) * height, :], inverse)
 
         @pl.when(my_row == 0)
         def _():
-            first[:NB, :] = -inverse
+            quarters[0][:NB, :] = -inverse
 
 
 def weigh(block, panel):
     height = panel.shape[0]
-    quarter = jax.ShapeDtypeStruct((height // 4, NB), jnp.float32)
-    half = jax.ShapeDtypeStruct((height // 2, NB), jnp.float32)
+    quarter = jax.ShapeDtypeStruct((height // N_PART, NB), jnp.float32)
     return pl.pallas_call(
         weigh_kernel,
-        out_shape=(quarter, quarter, half),
+        out_shape=(quarter,) * N_PART,
         in_specs=[VMEM, ANY],
-        out_specs=(VMEM, VMEM, VMEM),
+        out_specs=(VMEM,) * N_PART,
         scratch_shapes=[pltpu.VMEM((height, NB), jnp.float32), pltpu.SemaphoreType.DMA],
         compiler_params=SMALL,
         name="weigh",
@@ -373,44 +372,37 @@
     return c, mine, other
 
 
-def update_kernel(late, mine, theirs, factors, base, *refs):
-    out, buffer, sems = refs[-3:]
+def update_kernel(mine, late, piece, factors, base, *refs):
+    out, buffer, sem = refs[-3:]
     core, my_bit, other_bit = holdings()
-    height = mine.shape[0]
-    quarters = (2 * core + (my_bit ^ late), 2 * (1 - core) + (other_bit ^ late))
-    copies = []
-    for s, (piece, quarter) in enumerate(zip((mine, theirs), quarters)):
-        start = pl.multiple_of(quarter * height, height)
-        first, second, third = split(piece[...])
-        lead = jnp.concatenate([first, second], axis=1)
-        tail = jnp.concatenate([first, third], axis=1)
-        product = functools.partial(jnp.dot, preferred_element_type=jnp.float32)
-        total = product(tail, factors[2]) + product(lead, factors[1]) + product(lead, factors[0])
-        buffer[s] = base[pl.ds(start, height), :] - total
-        copy = pltpu.make_async_copy(buffer.at[s], out.at[pl.ds(start, height), :], sems.at[s])
-        copy.start()
-        copies.append(copy)
-    for copy in copies:
-        copy.wait()
-
-
-def update(late, mine, theirs, factors, base, done):
-    height, cols = mine.shape[0], base.shape[1]
+    height = piece.shape[0]
+    quarter = 2 * core + (my_bit ^ late) if mine else 2 * (1 - core) + (other_bit ^ late)
+    start = pl.multiple_of(quarter * height, height)
+    first, second, third = split(piece[...])
+    lead = jnp.concatenate([first, second], axis=1)
+    tail = jnp.concatenate([first, third], axis=1)
+    product = functools.partial(jnp.dot, preferred_element_type=jnp.float32)
+    total = product(tail, factors[2]) + product(lead, factors[1]) + product(lead, factors[0])
+    buffer[...] = base[pl.ds(start, height), :] - total
+    copy = pltpu.make_async_copy(buffer, out.at[pl.ds(start, height), :], sem)
+    copy.start()
+    copy.wait()
+
+
+def update(mine, late, piece, factors, base, done):
+    height, cols = piece.shape[0], base.shape[1]
     extra = [] if done is None else [done]
     return pl.pallas_call(
-        functools.partial(update_kernel, late),
+        functools.partial(update_kernel, mine, late),
         out_shape=jax.ShapeDtypeStruct(base.shape, jnp.float32),
-        in_specs=[VMEM] * 4 + [ANY] * len(extra),
+        in_specs=[VMEM] * 3 + [ANY] * len(extra),
         out_specs=ANY,
-        scratch_shapes=[
-            pltpu.VMEM((2, height, cols), jnp.float32),
-            pltpu.SemaphoreType.DMA((2,)),
-        ],
-        input_output_aliases={4: 0} if extra else {},
+        scratch_shapes=[pltpu.VMEM((height, cols), jnp.float32), pltpu.SemaphoreType.DMA],
+        input_output_aliases={3: 0} if extra else {},
         compiler_params=SMALL,
-        cost_estimate=pl.CostEstimate(flops=0, bytes_accessed=4 << 20, transcendentals=0),
+        cost_estimate=pl.CostEstimate(flops=0, bytes_accessed=2 << 20, transcendentals=0),
         name="update",
-    )(mine, theirs, factors, base, *extra)
+    )(piece, factors, base, *extra)
 
 
 def blank_kernel(out):
@@ -445,25 +437,28 @@
     zl, y = (lax.axis_index(name) for name in ROWS)
     panel = lax.optimization_barrier(matrix[:, :NB])
     lower = panel[:NB]
-    got = send_rows(lower, [((0, 0), (1, 0))])
+    targets = ((1, 0), (0, 1), (0, 3))
+    received = [send_rows(lower, [((0, 0), t)]) for t in targets]
     plan = make_plan(pivot_rows.reshape(1, NB))
-    lower = jnp.where(zl == 1, after(got, plan), lower)
-    got = send_rows(lower, [((a, 0), (a, 1)) for a in (0, 1)])
-    sent = pack(jnp.zeros((1,), jnp.int32), after(plan, lower), matrix)
-    lower = jnp.where(y == 1, after(got, sent), lower)
-    got = send_rows(lower, [((a, s), (a, t)) for a in (0, 1) for s, t in ((0, 3), (1, 2))])
-    lower = jnp.where(y >= 2, got, lower)
+    sent = pack(jnp.zeros((1,), jnp.int32), plan, matrix)
+    *received, sent = lax.optimization_barrier((*received, sent))
+    for (a, b), got in zip(targets, received):
+        lower = jnp.where((zl == a) & (y == b), got, lower)
+    got = send_rows(
+        lower, [((0, 0), (0, 2)), ((1, 0), (1, 2)), ((0, 1), (1, 1)), ((0, 3), (1, 3))]
+    )
+    lower = jnp.where((y == 2) | ((zl == 1) & (y != 0)), got, lower)
     rows = lax.all_to_all(after(sent, lower), ROWS, 0, 0)
     rest = later_rounds(after(plan, sent), matrix)
-    first, second, half = weigh(lower, panel)
+    quarters = weigh(lower, panel)
 
     zs, xs = range(N_ZH), range(N_X)
-    quarter = matrix.shape[0] // N_PART
-    got = send_cols(half, [((0, 0, 0), (0, 0, 1))])
-    first = jnp.where(c == 0, first, got[:quarter])
-    second = jnp.where(c == 0, second, got[quarter:])
-    got = send_cols(second, [((0, 0, 0), (0, 1, 0)), ((0, 0, 1), (0, 3, 1))])
-    piece = jnp.where(x == jnp.where(c == 0, 1, 3), got, first)
+    to_near = send_cols(quarters[1], [((0, 0, 0), (0, 1, 0))])
+    to_far = send_cols(quarters[3], [((0, 0, 0), (0, 3, 1))])
+    to_core = send_cols(quarters[2], [((0, 0, 0), (0, 0, 1))])
+    piece = jnp.where(
+        c == 0, jnp.where(x == 1, to_near, quarters[0]), jnp.where(x == 3, to_far, to_core)
+    )
     got = send_cols(
         piece,
         [((0, s, 0), (0, t, 0)) for s, t in ((0, 3), (1, 2))]
@@ -484,20 +479,19 @@
     got = after(got, factors)
     piece = jnp.where((zh == 2) | (zh == jnp.where(c == 0, 3, 1)), got, piece)
     chips = [(b, a) for a in xs for b in zs]
-    other = send_cols(piece, [((b, a, d), (b, a, 1 - d)) for b, a in chips for d in (0, 1)])
+    swap = [((b, a, d), (b, a, 1 - d)) for b, a in chips for d in (0, 1)]
     across = send_cols(
         piece,
         [((b, a, 0), (b, NEAR[a], 0)) for b, a in chips]
         + [((b, a, 1), (b, FAR[a], 1)) for b, a in chips],
     )
-    crossed = send_cols(
-        piece,
-        [((b, a, 0), (b, NEAR[a], 1)) for b, a in chips]
-        + [((b, a, 1), (b, FAR[a], 0)) for b, a in chips],
-    )
-    out = update(0, piece, other, factors, base, None)
-    across, crossed, out = lax.optimization_barrier((across, crossed, out))
-    return update(1, across, crossed, factors, base, out)
+    other = send_cols(piece, swap)
+    out = update(True, 0, piece, factors, base, None)
+    out = update(False, 0, other, factors, base, out)
+    across, out = lax.optimization_barrier((across, out))
+    other_across = send_cols(across, swap)
+    out = update(True, 1, across, factors, base, out)
+    return update(False, 1, other_across, factors, base, out)
 
 
 def solution(mesh):

time: 57.4 us -> 54.2 us (0.944)
  the two profiles are of different devices: /device:TPU:169 before, /device:TPU:161 now
where the time goes in v3:
time: 54.2 us; the launch traced here: 53.7 us
  starting transfers between devices  22.7 us (42%)
  waiting for transfers between devices  16.8 us (31%)
  Pallas kernels  11 us (20%)
  local copies, waits for them, and re-layouts  2.22 us (4%)
  loops' own time  0.55 us (1%)
    all_to_all x1, waiting for transfers between devices, local(): rows = lax.all_to_all(after(sent, lower), ROWS, 0, 0)  14.8 us
    ppermute x9, starting transfers between devices, send_cols(): lax.ppermute(value, COLS, [(pcol_id(*s), pcol_id(*t)) for s, t in pairs])  9.81 us
    ppermute x4, starting transfers between devices, send_rows(): return lax.ppermute(value, ROWS + COLS, pairs)  6.82 us
    all_to_all x1, starting transfers between devices, local(): rows = lax.all_to_all(after(sent, lower), ROWS, 0, 0)  6.06 us
    pallas_call x4, Pallas kernels, update(): pl.pallas_call(functools.partial(update_kernel, mine, late), out_shape=ja...  5.52 us
    pallas_call x1, Pallas kernels, pack(): pl.pallas_call(pack_kernel, out_shape=jax.ShapeDtypeStruct((N_PROW, 2 * S...  3.19 us
    pallas_call x1, Pallas kernels, prepare(): pl.pallas_call(prepare_kernel, out_shape=(jax.ShapeDtypeStruct(matrix.sha...  2.06 us
    ppermute x4, waiting for transfers between devices, send_rows(): return lax.ppermute(value, ROWS + COLS, pairs)  1.31 us
  transfers between devices with their start and end apart: 14, of which 3 were waited for; matrix products, arithmetic and copies ran while one was open for 1% of the time, Pallas kernels for 18%

profile of v3, /device:TPU:161, one launch (start us, length us, event | category | flops | bytes accessed | tf_op | source)
XLA Modules:
  0.0 53.7 jit_solution(14944669724131711879)
XLA Ops:
  0.0 1.1 %slice.9.panel_hbm = f32[1024,128]{1,0:T(8,128)S(1)} slice(f32[1024,768]{1,0:T(8,128)} %matrix.3), slice={[0:1024], [0:128]} | slice | bytes 1048576 | tf_op jit(solution)/shard_map/slice | solution.py:438
  1.1 1.3 %collective-permute-start = (f32[128,128]{1,0:T(8,128)S(1)}, f32[128,128]{1,0:T(8,128)S(1)}, u32[]{:S(2)}, u32[]{:S(2)}) collective-permute-start(f32[128,128]{1,0:T(8,128)S(1)} %slice.12), channel_id=1, source_target_pairs={{0,128},{1,129},{2,130},{3,131},{4,132},{5,133},{6,134},{7,135},{8... | collective-permute-start | bytes 196616 | tf_op jit(solution)/shard_map/ppermute | solution.py:55
  2.4 0.7 %collective-permute-start.1 = (f32[128,128]{1,0:T(8,128)S(1)}, f32[128,128]{1,0:T(8,128)S(1)}, u32[]{:S(2)}, u32[]{:S(2)}) collective-permute-start(f32[128,128]{1,0:T(8,128)S(1)} %slice.12), channel_id=1, source_target_pairs={{0,32},{1,33},{2,34},{3,35},{4,36},{5,37},{6,38},{7,39},{8,40},{9,... | collective-permute-start | bytes 196616 | tf_op jit(solution)/shard_map/ppermute | solution.py:55
  3.1 0.7 %collective-permute-start.2 = (f32[128,128]{1,0:T(8,128)S(1)}, f32[128,128]{1,0:T(8,128)S(1)}, u32[]{:S(2)}, u32[]{:S(2)}) collective-permute-start(f32[128,128]{1,0:T(8,128)S(1)} %slice.12), channel_id=1, source_target_pairs={{0,96},{1,97},{2,98},{3,99},{4,100},{5,101},{6,102},{7,103},{8,104... | collective-permute-start | bytes 196616 | tf_op jit(solution)/shard_map/ppermute | solution.py:55
  3.8 0.6 %copy-done = s32[128]{0:T(128)S(1)} copy-done((s32[128]{0:T(128)S(1)}, s32[128]{0:T(128)}, u32[]{:S(2)}) %copy-start) | copy-done | bytes 536
  4.6 3.2 %pack.8 = f32[8,64,768]{2,1,0:T(8,128)} custom-call(s32[1]{0:T(128)} %constant.63.clone.1.turn, s32[8,128]{1,0:T(8,128)S(1)} %plan.1.plan_hbm, f32[1024,768]{1,0:T(8,128)} %matrix.3), custom_call_target="tpu_custom_call" | custom-call | bytes 6291456 | tf_op jit(solution)/shard_map/pack/pallas_call | solution.py:176
  7.9 4.2 %collective-permute-start.3 = (f32[128,128]{1,0:T(8,128)S(1)}, f32[128,128]{1,0:T(8,128)S(1)}, u32[]{:S(2)}, u32[]{:S(2)}) collective-permute-start(f32[128,128]{1,0:T(8,128)S(1)} %select_select_fusion.1), channel_id=1, source_target_pairs={{0,64},{1,65},{2,66},{3,67},{4,68},{5,69},{6,70},{7,71},{8,72},{9,... | collective-permute-start | bytes 196616 | tf_op jit(solution)/shard_map/ppermute | solution.py:55
  12.1 1.3 %collective-permute-done.3 = f32[128,128]{1,0:T(8,128)S(1)} collective-permute-done((f32[128,128]{1,0:T(8,128)S(1)}, f32[128,128]{1,0:T(8,128)S(1)}, u32[]{:S(2)}, u32[]{:S(2)}) %collective-permute-start.3) | collective-permute-done | bytes 65568 | tf_op jit(solution)/shard_map/ppermute | solution.py:55
  13.4 6.1 %all-to-all-start.1 = ((f32[8,64,768]{2,1,0:T(8,128)}), f32[8,64,768]{2,1,0:T(8,128)S(1)}, u32[]{:S(2)}, u32[]{:S(2)}) async-start(f32[8,64,768]{2,1,0:T(8,128)} %pack.8), calls=%async_computation.1 | async-start | bytes 3145728 | tf_op jit(solution)/shard_map/all_to_all | solution.py:451
  19.5 0.7 %collective-permute-start.4 = (f32[256,128]{1,0:T(8,128)S(1)}, f32[256,128]{1,0:T(8,128)S(1)}, u32[]{:S(2)}, u32[]{:S(2)}) collective-permute-start(f32[256,128]{1,0:T(8,128)S(1)} %get-tuple-element.130), channel_id=1, source_target_pairs={{0,2},{32,34},{64,66},{96,98},{128,130},{160,162},{192,194},{224,2... | collective-permute-start | bytes 393224 | tf_op jit(solution)/shard_map/ppermute | solution.py:50
  20.2 0.7 %collective-permute-start.5 = (f32[256,128]{1,0:T(8,128)S(1)}, f32[256,128]{1,0:T(8,128)S(1)}, u32[]{:S(2)}, u32[]{:S(2)}) collective-permute-start(f32[256,128]{1,0:T(8,128)S(1)} %get-tuple-element.132), channel_id=1, source_target_pairs={{0,7},{32,39},{64,71},{96,103},{128,135},{160,167},{192,199},{224,... | collective-permute-start | bytes 393224 | tf_op jit(solution)/shard_map/ppermute | solution.py:50
  20.9 0.7 %collective-permute-start.6 = (f32[256,128]{1,0:T(8,128)S(1)}, f32[256,128]{1,0:T(8,128)S(1)}, u32[]{:S(2)}, u32[]{:S(2)}) collective-permute-start(f32[256,128]{1,0:T(8,128)S(1)} %get-tuple-element.133), channel_id=1, source_target_pairs={{0,1},{32,33},{64,65},{96,97},{128,129},{160,161},{192,193},{224,2... | collective-permute-start | bytes 393224 | tf_op jit(solution)/shard_map/ppermute | solution.py:50
  21.6 0.7 %collective-permute-start.7 = (f32[256,128]{1,0:T(8,128)S(1)}, f32[256,128]{1,0:T(8,128)S(1)}, u32[]{:S(2)}, u32[]{:S(2)}) collective-permute-start(f32[256,128]{1,0:T(8,128)S(1)} %select_select_fusion), channel_id=1, source_target_pairs={{0,6},{2,4},{1,3},{7,5},{32,38},{34,36},{33,35},{39,37},{64,70},{6... | collective-permute-start | bytes 393224 | tf_op jit(solution)/shard_map/ppermute | solution.py:50
  22.3 0.7 %collective-permute-start.8 = (f32[256,128]{1,0:T(8,128)S(1)}, f32[256,128]{1,0:T(8,128)S(1)}, u32[]{:S(2)}, u32[]{:S(2)}) collective-permute-start(f32[256,128]{1,0:T(8,128)S(1)} %broadcast_select_fusion), channel_id=1, source_target_pairs={{0,8},{2,10},{4,12},{6,14},{1,25},{3,27},{5,29},{7,31},{32,40},{34... | collective-permute-start | bytes 393224 | tf_op jit(solution)/shard_map/ppermute | solution.py:50
  23.6 1.3 %collective-permute-start.9 = (f32[256,128]{1,0:T(8,128)S(1)}, f32[256,128]{1,0:T(8,128)S(1)}, u32[]{:S(2)}, u32[]{:S(2)}) collective-permute-start(f32[256,128]{1,0:T(8,128)S(1)} %broadcast_select_fusion.1), channel_id=1, source_target_pairs={{0,24},{8,16},{2,26},{10,18},{4,28},{12,20},{6,30},{14,22},{1,9},{... | collective-permute-start | bytes 393224 | tf_op jit(solution)/shard_map/ppermute | solution.py:50
  24.9 14.8 %all-to-all-done.1.rows = f32[8,64,768]{2,1,0:T(8,128)S(1)} async-done(((f32[8,64,768]{2,1,0:T(8,128)}), f32[8,64,768]{2,1,0:T(8,128)S(1)}, u32[]{:S(2)}, u32[]{:S(2)}) %all-to-all-start.1) | async-done | bytes 1572896 | tf_op jit(solution)/shard_map/all_to_all | solution.py:451
  39.7 0.6 %while.14 = (s32[]{:T(128)}, f32[3,8,64,768]{3,2,1,0:T(8,128)}, s32[]{:T(128)}, s32[8,128]{1,0:T(8,128)S(1)}, f32[1024,768]{1,0:T(8,128)}, /*index=5*/s32[]{:T(128)}, s32[]{:T(128)}, s32[]{:T(128)}, s32[]{:T(128)}) while((s32[]{:T(128)}, f32[3,8,64,768]{3,2,1,0:T(8,128)}, s32[]{:T(128)}, s32[8,128]{1,0:T(8,128)S(1)}, f32[1024,768]{1,0:T(8,128)}, ...), condition=%wide.region_1.2_spmd, body=%wide.region_0.1_spmd.sunk | while | flops 7 | bytes 14155963 | solution.py:432
  40.3 2.1 %prepare.1 = (f32[1024,768]{1,0:T(8,128)S(1)}, bf16[3,256,768]{2,1,0:T(8,128)(2,1)S(1)}) custom-call(s32[8,128]{1,0:T(8,128)S(1)} %get-tuple-element.233, f32[8,64,768]{2,1,0:T(8,128)S(1)} %all-to-all-done.1.rows, f32[3,8,64,768]{3,2,1,0:T(8,128)} %get-tuple-element.138.rest, f32[1024,768]{1,0:T(8,128)} %get-tuple-element.223), custom_call_target="tpu_custom_call" | custom-call | bytes 9437184 | tf_op jit(solution)/shard_map/prepare/pallas_call | solution.py:347
  42.3 0.6 %collective-permute-done.9 = f32[256,128]{1,0:T(8,128)S(1)} collective-permute-done((f32[256,128]{1,0:T(8,128)S(1)}, f32[256,128]{1,0:T(8,128)S(1)}, u32[]{:S(2)}, u32[]{:S(2)}) %collective-permute-start.9) | collective-permute-done | bytes 131104 | tf_op jit(solution)/shard_map/ppermute | solution.py:50
  43.3 4.7 %collective-permute-start.10 = (f32[256,128]{1,0:T(8,128)S(1)}, f32[256,128]{1,0:T(8,128)S(1)}, u32[]{:S(2)}, u32[]{:S(2)}) collective-permute-start(f32[256,128]{1,0:T(8,128)S(1)} %broadcast_select_fusion.2.piece), channel_id=1, source_target_pairs={{0,2},{8,10},{16,18},{24,26},{2,0},{10,8},{18,16},{26,24},{4,6},{1... | collective-permute-start | bytes 393224 | tf_op jit(solution)/shard_map/ppermute | solution.py:50
  48.1 1.4 %update.4.refs_0_ = f32[1024,768]{1,0:T(8,128)} custom-call(f32[256,128]{1,0:T(8,128)S(1)} %broadcast_select_fusion.2.piece, bf16[3,256,768]{2,1,0:T(8,128)(2,1)S(1)} %get-tuple-element.139.factors, f32[1024,768]{1,0:T(8,128)S(1)} %get-tuple-element.141.base), custom_call_target="tpu_custom_call" | custom-call | bytes 2097152 | tf_op jit(solution)/shard_map/update/pallas_call | solution.py:395
  49.4 1.4 %update.5.refs_0_ = f32[1024,768]{1,0:T(8,128)} custom-call(f32[256,128]{1,0:T(8,128)S(1)} %collective-permute-done.11.piece, bf16[3,256,768]{2,1,0:T(8,128)(2,1)S(1)} %get-tuple-element.139.factors, f32[1024,768]{1,0:T(8,128)S(1)} %get-tuple-element.141.base, f32[1024,768]{1,0:T(8,128)} %update.4.refs_0_), custom_call_target="tpu_custom_call", output_to_operand_aliasing={{}: (3, {})} | custom-call | bytes 2097152 | tf_op jit(solution)/shard_map/update/pallas_call | solution.py:395
  50.9 1.4 %update.6.refs_0_ = f32[1024,768]{1,0:T(8,128)} custom-call(f32[256,128]{1,0:T(8,128)S(1)} %collective-permute-done.10.piece, bf16[3,256,768]{2,1,0:T(8,128)(2,1)S(1)} %get-tuple-element.139.factors, f32[1024,768]{1,0:T(8,128)S(1)} %get-tuple-element.141.base, f32[1024,768]{1,0:T(8,128)} %update.5.refs_0_), custom_call_target="tpu_custom_call", output_to_operand_aliasing={{}: (3, {})} | custom-call | bytes 2097152 | tf_op jit(solution)/shard_map/update/pallas_call | solution.py:395
  52.3 1.4 %update.7 = f32[1024,768]{1,0:T(8,128)} custom-call(f32[256,128]{1,0:T(8,128)S(1)} %collective-permute-done.12.piece, bf16[3,256,768]{2,1,0:T(8,128)(2,1)S(1)} %get-tuple-element.139.factors, f32[1024,768]{1,0:T(8,128)S(1)} %get-tuple-element.141.base, f32[1024,768]{1,0:T(8,128)} %update.6.refs_0_), custom_call_target="tpu_custom_call", output_to_operand_aliasing={{}: (3, {})} | custom-call | bytes 2097152 | tf_op jit(solution)/shard_map/update/pallas_call | solution.py:395
  (25 shorter events, 1.3 us)
Async XLA Ops:
  1.1 6.8 %collective-permute-start = (f32[128,128]{1,0:T(8,128)S(1)}, f32[128,128]{1,0:T(8,128)S(1)}, u32[]{:S(2)}, u32[]{:S(2)}) collective-permute-start(f32[128,128]{1,0:T(8,128)S(1)} %slice.12), channel_id=1, source_target_pairs={{0,128},{1,129},{2,130},{3,131},{4,132},{5,133},{6,134},{7,135},{8... | collective-permute-start | bytes 196616 | tf_op jit(solution)/shard_map/ppermute | solution.py:55
  2.4 5.5 %collective-permute-start.1 = (f32[128,128]{1,0:T(8,128)S(1)}, f32[128,128]{1,0:T(8,128)S(1)}, u32[]{:S(2)}, u32[]{:S(2)}) collective-permute-start(f32[128,128]{1,0:T(8,128)S(1)} %slice.12), channel_id=1, source_target_pairs={{0,32},{1,33},{2,34},{3,35},{4,36},{5,37},{6,38},{7,39},{8,40},{9,... | collective-permute-start | bytes 196616 | tf_op jit(solution)/shard_map/ppermute | solution.py:55
  3.1 4.8 %collective-permute-start.2 = (f32[128,128]{1,0:T(8,128)S(1)}, f32[128,128]{1,0:T(8,128)S(1)}, u32[]{:S(2)}, u32[]{:S(2)}) collective-permute-start(f32[128,128]{1,0:T(8,128)S(1)} %slice.12), channel_id=1, source_target_pairs={{0,96},{1,97},{2,98},{3,99},{4,100},{5,101},{6,102},{7,103},{8,104... | collective-permute-start | bytes 196616 | tf_op jit(solution)/shard_map/ppermute | solution.py:55
  3.8 0.7 %copy-start = (s32[128]{0:T(128)S(1)}, s32[128]{0:T(128)}, u32[]{:S(2)}) copy-start(s32[128]{0:T(128)} %param.5) | copy-start | bytes 1540
  7.9 5.5 %collective-permute-start.3 = (f32[128,128]{1,0:T(8,128)S(1)}, f32[128,128]{1,0:T(8,128)S(1)}, u32[]{:S(2)}, u32[]{:S(2)}) collective-permute-start(f32[128,128]{1,0:T(8,128)S(1)} %select_select_fusion.1), channel_id=1, source_target_pairs={{0,64},{1,65},{2,66},{3,67},{4,68},{5,69},{6,70},{7,71},{8,72},{9,... | collective-permute-start | bytes 196616 | tf_op jit(solution)/shard_map/ppermute | solution.py:55
  13.4 26.3 %all-to-all-start.1 = ((f32[8,64,768]{2,1,0:T(8,128)}), f32[8,64,768]{2,1,0:T(8,128)S(1)}, u32[]{:S(2)}, u32[]{:S(2)}) async-start(f32[8,64,768]{2,1,0:T(8,128)} %pack.8), calls=%async_computation.1 | async-start | bytes 3145728 | tf_op jit(solution)/shard_map/all_to_all | solution.py:451
  19.5 2.0 %collective-permute-start.4 = (f32[256,128]{1,0:T(8,128)S(1)}, f32[256,128]{1,0:T(8,128)S(1)}, u32[]{:S(2)}, u32[]{:S(2)}) collective-permute-start(f32[256,128]{1,0:T(8,128)S(1)} %get-tuple-element.130), channel_id=1, source_target_pairs={{0,2},{32,34},{64,66},{96,98},{128,130},{160,162},{192,194},{224,2... | collective-permute-start | bytes 393224 | tf_op jit(solution)/shard_map/ppermute | solution.py:50
  20.2 1.4 %collective-permute-start.5 = (f32[256,128]{1,0:T(8,128)S(1)}, f32[256,128]{1,0:T(8,128)S(1)}, u32[]{:S(2)}, u32[]{:S(2)}) collective-permute-start(f32[256,128]{1,0:T(8,128)S(1)} %get-tuple-element.132), channel_id=1, source_target_pairs={{0,7},{32,39},{64,71},{96,103},{128,135},{160,167},{192,199},{224,... | collective-permute-start | bytes 393224 | tf_op jit(solution)/shard_map/ppermute | solution.py:50
  20.9 0.7 %collective-permute-start.6 = (f32[256,128]{1,0:T(8,128)S(1)}, f32[256,128]{1,0:T(8,128)S(1)}, u32[]{:S(2)}, u32[]{:S(2)}) collective-permute-start(f32[256,128]{1,0:T(8,128)S(1)} %get-tuple-element.133), channel_id=1, source_target_pairs={{0,1},{32,33},{64,65},{96,97},{128,129},{160,161},{192,193},{224,2... | collective-permute-start | bytes 393224 | tf_op jit(solution)/shard_map/ppermute | solution.py:50
  21.6 0.7 %collective-permute-start.7 = (f32[256,128]{1,0:T(8,128)S(1)}, f32[256,128]{1,0:T(8,128)S(1)}, u32[]{:S(2)}, u32[]{:S(2)}) collective-permute-start(f32[256,128]{1,0:T(8,128)S(1)} %select_select_fusion), channel_id=1, source_target_pairs={{0,6},{2,4},{1,3},{7,5},{32,38},{34,36},{33,35},{39,37},{64,70},{6... | collective-permute-start | bytes 393224 | tf_op jit(solution)/shard_map/ppermute | solution.py:50
  22.3 1.2 %collective-permute-start.8 = (f32[256,128]{1,0:T(8,128)S(1)}, f32[256,128]{1,0:T(8,128)S(1)}, u32[]{:S(2)}, u32[]{:S(2)}) collective-permute-start(f32[256,128]{1,0:T(8,128)S(1)} %broadcast_select_fusion), channel_id=1, source_target_pairs={{0,8},{2,10},{4,12},{6,14},{1,25},{3,27},{5,29},{7,31},{32,40},{34... | collective-permute-start | bytes 393224 | tf_op jit(solution)/shard_map/ppermute | solution.py:50
  23.6 19.4 %collective-permute-start.9 = (f32[256,128]{1,0:T(8,128)S(1)}, f32[256,128]{1,0:T(8,128)S(1)}, u32[]{:S(2)}, u32[]{:S(2)}) collective-permute-start(f32[256,128]{1,0:T(8,128)S(1)} %broadcast_select_fusion.1), channel_id=1, source_target_pairs={{0,24},{8,16},{2,26},{10,18},{4,28},{12,20},{6,30},{14,22},{1,9},{... | collective-permute-start | bytes 393224 | tf_op jit(solution)/shard_map/ppermute | solution.py:50
  43.0 6.5 %collective-permute-start.11 = (f32[256,128]{1,0:T(8,128)S(1)}, f32[256,128]{1,0:T(8,128)S(1)}, u32[]{:S(2)}, u32[]{:S(2)}) collective-permute-start(f32[256,128]{1,0:T(8,128)S(1)} %broadcast_select_fusion.2.piece), channel_id=1, source_target_pairs={{0,1},{1,0},{8,9},{9,8},{16,17},{17,16},{24,25},{25,24},{2,3},{3,2... | collective-permute-start | bytes 393224 | tf_op jit(solution)/shard_map/ppermute | solution.py:50
  43.3 7.5 %collective-permute-start.10 = (f32[256,128]{1,0:T(8,128)S(1)}, f32[256,128]{1,0:T(8,128)S(1)}, u32[]{:S(2)}, u32[]{:S(2)}) collective-permute-start(f32[256,128]{1,0:T(8,128)S(1)} %broadcast_select_fusion.2.piece), channel_id=1, source_target_pairs={{0,2},{8,10},{16,18},{24,26},{2,0},{10,8},{18,16},{26,24},{4,6},{1... | collective-permute-start | bytes 393224 | tf_op jit(solution)/shard_map/ppermute | solution.py:50
  50.8 1.5 %collective-permute-start.12 = (f32[256,128]{1,0:T(8,128)S(1)}, f32[256,128]{1,0:T(8,128)S(1)}, u32[]{:S(2)}, u32[]{:S(2)}) collective-permute-start(f32[256,128]{1,0:T(8,128)S(1)} %collective-permute-done.10.piece), channel_id=1, source_target_pairs={{0,1},{1,0},{8,9},{9,8},{16,17},{17,16},{24,25},{25,24},{2,3},{3,2... | collective-permute-start | bytes 393224 | tf_op jit(solution)/shard_map/ppermute | solution.py:50

commit v4 on v3

--- a/solution.py
+++ b/solution.py
@@ -52,6 +52,18 @@
 
 def send_rows(value, pairs, cols=range(N_PCOL)):
     pairs = [(prow_id(*s) * N_PCOL + q, prow_id(*t) * N_PCOL + q) for s, t in pairs for q in cols]
+    return lax.ppermute(value, ROWS + COLS, pairs)
+
+
+def send_along_zh(value, routes):
+    pairs = []
+    for zl in range(2):
+        for y in range(N_Y):
+            for a in range(N_X):
+                for d in range(N_C):
+                    for s, t in routes[zl ^ d]:
+                        row = prow_id(zl, y) * N_PCOL
+                        pairs.append((row + pcol_id(s, a, d), row + pcol_id(t, a, d)))
     return lax.ppermute(value, ROWS + COLS, pairs)
 
 
@@ -438,15 +450,16 @@
     panel = lax.optimization_barrier(matrix[:, :NB])
     lower = panel[:NB]
     targets = ((1, 0), (0, 1), (0, 3))
-    received = [send_rows(lower, [((0, 0), t)]) for t in targets]
+    received = [send_rows(lower, [((0, 0), t)], [0]) for t in targets]
     plan = make_plan(pivot_rows.reshape(1, NB))
-    sent = pack(jnp.zeros((1,), jnp.int32), plan, matrix)
-    *received, sent = lax.optimization_barrier((*received, sent))
+    *received, plan = lax.optimization_barrier((*received, plan))
     for (a, b), got in zip(targets, received):
         lower = jnp.where((zl == a) & (y == b), got, lower)
     got = send_rows(
-        lower, [((0, 0), (0, 2)), ((1, 0), (1, 2)), ((0, 1), (1, 1)), ((0, 3), (1, 3))]
+        lower, [((0, 0), (0, 2)), ((1, 0), (1, 2)), ((0, 1), (1, 1)), ((0, 3), (1, 3))], [0]
     )
+    sent = pack(jnp.zeros((1,), jnp.int32), after(plan, lower), matrix)
+    got, sent = lax.optimization_barrier((got, sent))
     lower = jnp.where((y == 2) | ((zl == 1) & (y != 0)), got, lower)
     rows = lax.all_to_all(after(sent, lower), ROWS, 0, 0)
     rest = later_rounds(after(plan, sent), matrix)
@@ -465,19 +478,13 @@
         + [((0, s, 1), (0, t, 1)) for s, t in ((0, 1), (3, 2))],
     )
     piece = jnp.where((x == 2) | (x == jnp.where(c == 0, 3, 1)), got, piece)
-    got = send_cols(
-        piece,
-        [((0, a, 0), (1, a, 0)) for a in xs] + [((0, a, 1), (3, a, 1)) for a in xs],
-    )
-    piece = jnp.where(zh == jnp.where(c == 0, 1, 3), got, piece)
+    upward = (c ^ zl) == 0
+    got = send_along_zh(piece, (((0, 1),), ((0, 3),)))
+    piece = jnp.where(zh == jnp.where(upward, 1, 3), got, piece)
     base, factors = prepare(plan, after(rows, piece), rest, matrix)
-    got = send_cols(
-        piece,
-        [((s, a, 0), (t, a, 0)) for a in xs for s, t in ((0, 3), (1, 2))]
-        + [((s, a, 1), (t, a, 1)) for a in xs for s, t in ((0, 1), (3, 2))],
-    )
+    got = send_along_zh(piece, (((0, 3), (1, 2)), ((0, 1), (3, 2))))
     got = after(got, factors)
-    piece = jnp.where((zh == 2) | (zh == jnp.where(c == 0, 3, 1)), got, piece)
+    piece = jnp.where((zh == 2) | (zh == jnp.where(upward, 3, 1)), got, piece)
     chips = [(b, a) for a in xs for b in zs]
     swap = [((b, a, d), (b, a, 1 - d)) for b, a in chips for d in (0, 1)]
     across = send_cols(

time: 54.2 us -> 52.1 us (0.961)
  the two profiles are of different devices: /device:TPU:161 before, /device:TPU:1 now
where the time goes in v4:
time: 52.1 us; the launch traced here: 51.5 us
  starting transfers between devices  21.9 us (42%)
  waiting for transfers between devices  15.2 us (29%)
  Pallas kernels  11.2 us (21%)
  local copies, waits for them, and re-layouts  2.22 us (4%)
  loops' own time  0.55 us (1%)
    ppermute x7, waiting for transfers between devices, send_cols(): lax.ppermute(value, COLS, [(pcol_id(*s), pcol_id(*t)) for s, t in pairs])  13.8 us
    ppermute x7, starting transfers between devices, send_cols(): lax.ppermute(value, COLS, [(pcol_id(*s), pcol_id(*t)) for s, t in pairs])  10.2 us
    all_to_all x1, starting transfers between devices, local(): rows = lax.all_to_all(after(sent, lower), ROWS, 0, 0)  6.46 us
    pallas_call x4, Pallas kernels, update(): pl.pallas_call(functools.partial(update_kernel, mine, late), out_shape=ja...  5.51 us
    pallas_call x1, Pallas kernels, pack(): pl.pallas_call(pack_kernel, out_shape=jax.ShapeDtypeStruct((N_PROW, 2 * S...  3.33 us
    ppermute x4, starting transfers between devices, send_rows(): return lax.ppermute(value, ROWS + COLS, pairs)  2.66 us
    ppermute x2, starting transfers between devices, send_along_zh(): return lax.ppermute(value, ROWS + COLS, pairs)  2.59 us
    pallas_call x1, Pallas kernels, prepare(): pl.pallas_call(prepare_kernel, out_shape=(jax.ShapeDtypeStruct(matrix.sha...  2.14 us
  transfers between devices with their start and end apart: 14, of which 3 were waited for; matrix products, arithmetic and copies ran while one was open for 1% of the time, Pallas kernels for 19%

profile of v4, /device:TPU:1, one launch (start us, length us, event | category | flops | bytes accessed | tf_op | source)
XLA Modules:
  0.0 51.5 jit_solution(15217137298231841794)
XLA Ops:
  0.0 1.1 %slice.9.panel_hbm = f32[1024,128]{1,0:T(8,128)S(1)} slice(f32[1024,768]{1,0:T(8,128)} %matrix.3), slice={[0:1024], [0:128]} | slice | bytes 1048576 | tf_op jit(solution)/shard_map/slice | solution.py:450
  1.1 0.7 %collective-permute-start.2 = (f32[128,128]{1,0:T(8,128)S(1)}, f32[128,128]{1,0:T(8,128)S(1)}, u32[]{:S(2)}, u32[]{:S(2)}) collective-permute-start(f32[128,128]{1,0:T(8,128)S(1)} %slice.12), channel_id=1, source_target_pairs={{0,96}} | collective-permute-start | bytes 196616 | tf_op jit(solution)/shard_map/ppermute | solution.py:55
  1.8 0.7 %collective-permute-start.1 = (f32[128,128]{1,0:T(8,128)S(1)}, f32[128,128]{1,0:T(8,128)S(1)}, u32[]{:S(2)}, u32[]{:S(2)}) collective-permute-start(f32[128,128]{1,0:T(8,128)S(1)} %slice.12), channel_id=1, source_target_pairs={{0,32}} | collective-permute-start | bytes 196616 | tf_op jit(solution)/shard_map/ppermute | solution.py:55
  2.4 0.7 %collective-permute-start = (f32[128,128]{1,0:T(8,128)S(1)}, f32[128,128]{1,0:T(8,128)S(1)}, u32[]{:S(2)}, u32[]{:S(2)}) collective-permute-start(f32[128,128]{1,0:T(8,128)S(1)} %slice.12), channel_id=1, source_target_pairs={{0,128}} | collective-permute-start | bytes 196616 | tf_op jit(solution)/shard_map/ppermute | solution.py:55
  3.1 0.6 %copy-done = s32[128]{0:T(128)S(1)} copy-done((s32[128]{0:T(128)S(1)}, s32[128]{0:T(128)}, u32[]{:S(2)}) %copy-start) | copy-done | bytes 536
  4.1 0.7 %collective-permute-start.3 = (f32[128,128]{1,0:T(8,128)S(1)}, f32[128,128]{1,0:T(8,128)S(1)}, u32[]{:S(2)}, u32[]{:S(2)}) collective-permute-start(f32[128,128]{1,0:T(8,128)S(1)} %select_select_fusion.1), channel_id=1, source_target_pairs={{0,64},{128,192},{32,160},{96,224}} | collective-permute-start | bytes 196616 | tf_op jit(solution)/shard_map/ppermute | solution.py:55
  4.8 3.3 %pack.8 = f32[8,64,768]{2,1,0:T(8,128)} custom-call(s32[1]{0:T(128)} %constant.63.clone.1.turn, s32[8,128]{1,0:T(8,128)S(1)} %plan.1.plan_hbm, f32[1024,768]{1,0:T(8,128)} %matrix.3), custom_call_target="tpu_custom_call" | custom-call | bytes 6291456 | tf_op jit(solution)/shard_map/pack/pallas_call | solution.py:188
  8.1 6.5 %all-to-all-start.1 = ((f32[8,64,768]{2,1,0:T(8,128)}), f32[8,64,768]{2,1,0:T(8,128)S(1)}, u32[]{:S(2)}, u32[]{:S(2)}) async-start(f32[8,64,768]{2,1,0:T(8,128)} %pack.8), calls=%async_computation.1 | async-start | bytes 3145728 | tf_op jit(solution)/shard_map/all_to_all | solution.py:464
  14.6 0.7 %collective-permute-start.4 = (f32[256,128]{1,0:T(8,128)S(1)}, f32[256,128]{1,0:T(8,128)S(1)}, u32[]{:S(2)}, u32[]{:S(2)}) collective-permute-start(f32[256,128]{1,0:T(8,128)S(1)} %get-tuple-element.136), channel_id=1, source_target_pairs={{0,2},{32,34},{64,66},{96,98},{128,130},{160,162},{192,194},{224,2... | collective-permute-start | bytes 393224 | tf_op jit(solution)/shard_map/ppermute | solution.py:50
  15.3 0.7 %collective-permute-start.5 = (f32[256,128]{1,0:T(8,128)S(1)}, f32[256,128]{1,0:T(8,128)S(1)}, u32[]{:S(2)}, u32[]{:S(2)}) collective-permute-start(f32[256,128]{1,0:T(8,128)S(1)} %get-tuple-element.138), channel_id=1, source_target_pairs={{0,7},{32,39},{64,71},{96,103},{128,135},{160,167},{192,199},{224,... | collective-permute-start | bytes 393224 | tf_op jit(solution)/shard_map/ppermute | solution.py:50
  16.0 1.3 %collective-permute-start.6 = (f32[256,128]{1,0:T(8,128)S(1)}, f32[256,128]{1,0:T(8,128)S(1)}, u32[]{:S(2)}, u32[]{:S(2)}) collective-permute-start(f32[256,128]{1,0:T(8,128)S(1)} %get-tuple-element.139), channel_id=1, source_target_pairs={{0,1},{32,33},{64,65},{96,97},{128,129},{160,161},{192,193},{224,2... | collective-permute-start | bytes 393224 | tf_op jit(solution)/shard_map/ppermute | solution.py:50
  17.3 11.8 %collective-permute-done.6 = f32[256,128]{1,0:T(8,128)S(1)} collective-permute-done((f32[256,128]{1,0:T(8,128)S(1)}, f32[256,128]{1,0:T(8,128)S(1)}, u32[]{:S(2)}, u32[]{:S(2)}) %collective-permute-start.6) | collective-permute-done | bytes 131104 | tf_op jit(solution)/shard_map/ppermute | solution.py:50
  29.2 1.3 %collective-permute-start.7 = (f32[256,128]{1,0:T(8,128)S(1)}, f32[256,128]{1,0:T(8,128)S(1)}, u32[]{:S(2)}, u32[]{:S(2)}) collective-permute-start(f32[256,128]{1,0:T(8,128)S(1)} %select_select_fusion), channel_id=1, source_target_pairs={{0,6},{2,4},{1,3},{7,5},{32,38},{34,36},{33,35},{39,37},{64,70},{6... | collective-permute-start | bytes 393224 | tf_op jit(solution)/shard_map/ppermute | solution.py:50
  30.5 1.9 %collective-permute-done.7 = f32[256,128]{1,0:T(8,128)S(1)} collective-permute-done((f32[256,128]{1,0:T(8,128)S(1)}, f32[256,128]{1,0:T(8,128)S(1)}, u32[]{:S(2)}, u32[]{:S(2)}) %collective-permute-start.7) | collective-permute-done | bytes 131104 | tf_op jit(solution)/shard_map/ppermute | solution.py:50
  32.4 1.3 %collective-permute-start.8 = (f32[256,128]{1,0:T(8,128)S(1)}, f32[256,128]{1,0:T(8,128)S(1)}, u32[]{:S(2)}, u32[]{:S(2)}) collective-permute-start(f32[256,128]{1,0:T(8,128)S(1)} %broadcast_select_fusion), channel_id=1, source_target_pairs={{0,8},{1,25},{2,10},{3,27},{4,12},{5,29},{6,14},{7,31},{32,40},{33... | collective-permute-start | bytes 393224 | tf_op jit(solution)/shard_map/ppermute | solution.py:67
  34.2 1.4 %collective-permute-done.8 = f32[256,128]{1,0:T(8,128)S(1)} collective-permute-done((f32[256,128]{1,0:T(8,128)S(1)}, f32[256,128]{1,0:T(8,128)S(1)}, u32[]{:S(2)}, u32[]{:S(2)}) %collective-permute-start.8) | collective-permute-done | bytes 131104 | tf_op jit(solution)/shard_map/ppermute | solution.py:67
  35.6 1.3 %collective-permute-start.9 = (f32[256,128]{1,0:T(8,128)S(1)}, f32[256,128]{1,0:T(8,128)S(1)}, u32[]{:S(2)}, u32[]{:S(2)}) collective-permute-start(f32[256,128]{1,0:T(8,128)S(1)} %broadcast_select_fusion.1), channel_id=1, source_target_pairs={{0,24},{8,16},{1,9},{25,17},{2,26},{10,18},{3,11},{27,19},{4,28},{... | collective-permute-start | bytes 393224 | tf_op jit(solution)/shard_map/ppermute | solution.py:67
  37.5 2.1 %prepare.1 = (f32[1024,768]{1,0:T(8,128)S(1)}, bf16[3,256,768]{2,1,0:T(8,128)(2,1)S(1)}) custom-call(s32[8,128]{1,0:T(8,128)S(1)} %get-tuple-element.239, f32[8,64,768]{2,1,0:T(8,128)S(1)} %all-to-all-done.1.rows, f32[3,8,64,768]{3,2,1,0:T(8,128)} %get-tuple-element.144.rest, f32[1024,768]{1,0:T(8,128)} %get-tuple-element.229), custom_call_target="tpu_custom_call" | custom-call | bytes 9437184 | tf_op jit(solution)/shard_map/prepare/pallas_call | solution.py:359
  39.7 2.8 %collective-permute-start.11 = (f32[256,128]{1,0:T(8,128)S(1)}, f32[256,128]{1,0:T(8,128)S(1)}, u32[]{:S(2)}, u32[]{:S(2)}) collective-permute-start(f32[256,128]{1,0:T(8,128)S(1)} %broadcast_select_fusion.2.piece), channel_id=1, source_target_pairs={{0,1},{1,0},{8,9},{9,8},{16,17},{17,16},{24,25},{25,24},{2,3},{3,2... | collective-permute-start | bytes 393224 | tf_op jit(solution)/shard_map/ppermute | solution.py:50
  42.5 3.4 %collective-permute-start.10 = (f32[256,128]{1,0:T(8,128)S(1)}, f32[256,128]{1,0:T(8,128)S(1)}, u32[]{:S(2)}, u32[]{:S(2)}) collective-permute-start(f32[256,128]{1,0:T(8,128)S(1)} %broadcast_select_fusion.2.piece), channel_id=1, source_target_pairs={{0,2},{8,10},{16,18},{24,26},{2,0},{10,8},{18,16},{26,24},{4,6},{1... | collective-permute-start | bytes 393224 | tf_op jit(solution)/shard_map/ppermute | solution.py:50
  45.9 1.4 %update.4.refs_0_ = f32[1024,768]{1,0:T(8,128)} custom-call(f32[256,128]{1,0:T(8,128)S(1)} %broadcast_select_fusion.2.piece, bf16[3,256,768]{2,1,0:T(8,128)(2,1)S(1)} %get-tuple-element.145.factors, f32[1024,768]{1,0:T(8,128)S(1)} %get-tuple-element.147.base), custom_call_target="tpu_custom_call" | custom-call | bytes 2097152 | tf_op jit(solution)/shard_map/update/pallas_call | solution.py:407
  47.3 1.4 %update.5.refs_0_ = f32[1024,768]{1,0:T(8,128)} custom-call(f32[256,128]{1,0:T(8,128)S(1)} %collective-permute-done.11.piece, bf16[3,256,768]{2,1,0:T(8,128)(2,1)S(1)} %get-tuple-element.145.factors, f32[1024,768]{1,0:T(8,128)S(1)} %get-tuple-element.147.base, f32[1024,768]{1,0:T(8,128)} %update.4.refs_0_), custom_call_target="tpu_custom_call", output_to_operand_aliasing={{}: (3, {})} | custom-call | bytes 2097152 | tf_op jit(solution)/shard_map/update/pallas_call | solution.py:407
  48.8 1.4 %update.6.refs_0_ = f32[1024,768]{1,0:T(8,128)} custom-call(f32[256,128]{1,0:T(8,128)S(1)} %collective-permute-done.10.piece, bf16[3,256,768]{2,1,0:T(8,128)(2,1)S(1)} %get-tuple-element.145.factors, f32[1024,768]{1,0:T(8,128)S(1)} %get-tuple-element.147.base, f32[1024,768]{1,0:T(8,128)} %update.5.refs_0_), custom_call_target="tpu_custom_call", output_to_operand_aliasing={{}: (3, {})} | custom-call | bytes 2097152 | tf_op jit(solution)/shard_map/update/pallas_call | solution.py:407
  50.2 1.4 %update.7 = f32[1024,768]{1,0:T(8,128)} custom-call(f32[256,128]{1,0:T(8,128)S(1)} %collective-permute-done.12.piece, bf16[3,256,768]{2,1,0:T(8,128)(2,1)S(1)} %get-tuple-element.145.factors, f32[1024,768]{1,0:T(8,128)S(1)} %get-tuple-element.147.base, f32[1024,768]{1,0:T(8,128)} %update.6.refs_0_), custom_call_target="tpu_custom_call", output_to_operand_aliasing={{}: (3, {})} | custom-call | bytes 2097152 | tf_op jit(solution)/shard_map/update/pallas_call | solution.py:407
  (25 shorter events, 1.5 us)
Async XLA Ops:
  1.1 2.9 %collective-permute-start.2 = (f32[128,128]{1,0:T(8,128)S(1)}, f32[128,128]{1,0:T(8,128)S(1)}, u32[]{:S(2)}, u32[]{:S(2)}) collective-permute-start(f32[128,128]{1,0:T(8,128)S(1)} %slice.12), channel_id=1, source_target_pairs={{0,96}} | collective-permute-start | bytes 196616 | tf_op jit(solution)/shard_map/ppermute | solution.py:55
  1.8 2.3 %collective-permute-start.1 = (f32[128,128]{1,0:T(8,128)S(1)}, f32[128,128]{1,0:T(8,128)S(1)}, u32[]{:S(2)}, u32[]{:S(2)}) collective-permute-start(f32[128,128]{1,0:T(8,128)S(1)} %slice.12), channel_id=1, source_target_pairs={{0,32}} | collective-permute-start | bytes 196616 | tf_op jit(solution)/shard_map/ppermute | solution.py:55
  2.4 1.6 %collective-permute-start = (f32[128,128]{1,0:T(8,128)S(1)}, f32[128,128]{1,0:T(8,128)S(1)}, u32[]{:S(2)}, u32[]{:S(2)}) collective-permute-start(f32[128,128]{1,0:T(8,128)S(1)} %slice.12), channel_id=1, source_target_pairs={{0,128}} | collective-permute-start | bytes 196616 | tf_op jit(solution)/shard_map/ppermute | solution.py:55
  3.1 0.7 %copy-start = (s32[128]{0:T(128)S(1)}, s32[128]{0:T(128)}, u32[]{:S(2)}) copy-start(s32[128]{0:T(128)} %param.5) | copy-start | bytes 1540
  4.1 4.0 %collective-permute-start.3 = (f32[128,128]{1,0:T(8,128)S(1)}, f32[128,128]{1,0:T(8,128)S(1)}, u32[]{:S(2)}, u32[]{:S(2)}) collective-permute-start(f32[128,128]{1,0:T(8,128)S(1)} %select_select_fusion.1), channel_id=1, source_target_pairs={{0,64},{128,192},{32,160},{96,224}} | collective-permute-start | bytes 196616 | tf_op jit(solution)/shard_map/ppermute | solution.py:55
  8.1 28.8 %all-to-all-start.1 = ((f32[8,64,768]{2,1,0:T(8,128)}), f32[8,64,768]{2,1,0:T(8,128)S(1)}, u32[]{:S(2)}, u32[]{:S(2)}) async-start(f32[8,64,768]{2,1,0:T(8,128)} %pack.8), calls=%async_computation.1 | async-start | bytes 3145728 | tf_op jit(solution)/shard_map/all_to_all | solution.py:464
  14.6 2.7 %collective-permute-start.4 = (f32[256,128]{1,0:T(8,128)S(1)}, f32[256,128]{1,0:T(8,128)S(1)}, u32[]{:S(2)}, u32[]{:S(2)}) collective-permute-start(f32[256,128]{1,0:T(8,128)S(1)} %get-tuple-element.136), channel_id=1, source_target_pairs={{0,2},{32,34},{64,66},{96,98},{128,130},{160,162},{192,194},{224,2... | collective-permute-start | bytes 393224 | tf_op jit(solution)/shard_map/ppermute | solution.py:50
  15.3 2.0 %collective-permute-start.5 = (f32[256,128]{1,0:T(8,128)S(1)}, f32[256,128]{1,0:T(8,128)S(1)}, u32[]{:S(2)}, u32[]{:S(2)}) collective-permute-start(f32[256,128]{1,0:T(8,128)S(1)} %get-tuple-element.138), channel_id=1, source_target_pairs={{0,7},{32,39},{64,71},{96,103},{128,135},{160,167},{192,199},{224,... | collective-permute-start | bytes 393224 | tf_op jit(solution)/shard_map/ppermute | solution.py:50
  16.0 13.2 %collective-permute-start.6 = (f32[256,128]{1,0:T(8,128)S(1)}, f32[256,128]{1,0:T(8,128)S(1)}, u32[]{:S(2)}, u32[]{:S(2)}) collective-permute-start(f32[256,128]{1,0:T(8,128)S(1)} %get-tuple-element.139), channel_id=1, source_target_pairs={{0,1},{32,33},{64,65},{96,97},{128,129},{160,161},{192,193},{224,2... | collective-permute-start | bytes 393224 | tf_op jit(solution)/shard_map/ppermute | solution.py:50
  29.2 3.2 %collective-permute-start.7 = (f32[256,128]{1,0:T(8,128)S(1)}, f32[256,128]{1,0:T(8,128)S(1)}, u32[]{:S(2)}, u32[]{:S(2)}) collective-permute-start(f32[256,128]{1,0:T(8,128)S(1)} %select_select_fusion), channel_id=1, source_target_pairs={{0,6},{2,4},{1,3},{7,5},{32,38},{34,36},{33,35},{39,37},{64,70},{6... | collective-permute-start | bytes 393224 | tf_op jit(solution)/shard_map/ppermute | solution.py:50
  32.4 3.2 %collective-permute-start.8 = (f32[256,128]{1,0:T(8,128)S(1)}, f32[256,128]{1,0:T(8,128)S(1)}, u32[]{:S(2)}, u32[]{:S(2)}) collective-permute-start(f32[256,128]{1,0:T(8,128)S(1)} %broadcast_select_fusion), channel_id=1, source_target_pairs={{0,8},{1,25},{2,10},{3,27},{4,12},{5,29},{6,14},{7,31},{32,40},{33... | collective-permute-start | bytes 393224 | tf_op jit(solution)/shard_map/ppermute | solution.py:67
  35.6 4.0 %collective-permute-start.9 = (f32[256,128]{1,0:T(8,128)S(1)}, f32[256,128]{1,0:T(8,128)S(1)}, u32[]{:S(2)}, u32[]{:S(2)}) collective-permute-start(f32[256,128]{1,0:T(8,128)S(1)} %broadcast_select_fusion.1), channel_id=1, source_target_pairs={{0,24},{8,16},{1,9},{25,17},{2,26},{10,18},{3,11},{27,19},{4,28},{... | collective-permute-start | bytes 393224 | tf_op jit(solution)/shard_map/ppermute | solution.py:67
  39.7 7.6 %collective-permute-start.11 = (f32[256,128]{1,0:T(8,128)S(1)}, f32[256,128]{1,0:T(8,128)S(1)}, u32[]{:S(2)}, u32[]{:S(2)}) collective-permute-start(f32[256,128]{1,0:T(8,128)S(1)} %broadcast_select_fusion.2.piece), channel_id=1, source_target_pairs={{0,1},{1,0},{8,9},{9,8},{16,17},{17,16},{24,25},{25,24},{2,3},{3,2... | collective-permute-start | bytes 393224 | tf_op jit(solution)/shard_map/ppermute | solution.py:50
  42.5 6.2 %collective-permute-start.10 = (f32[256,128]{1,0:T(8,128)S(1)}, f32[256,128]{1,0:T(8,128)S(1)}, u32[]{:S(2)}, u32[]{:S(2)}) collective-permute-start(f32[256,128]{1,0:T(8,128)S(1)} %broadcast_select_fusion.2.piece), channel_id=1, source_target_pairs={{0,2},{8,10},{16,18},{24,26},{2,0},{10,8},{18,16},{26,24},{4,6},{1... | collective-permute-start | bytes 393224 | tf_op jit(solution)/shard_map/ppermute | solution.py:50
  48.7 1.5 %collective-permute-start.12 = (f32[256,128]{1,0:T(8,128)S(1)}, f32[256,128]{1,0:T(8,128)S(1)}, u32[]{:S(2)}, u32[]{:S(2)}) collective-permute-start(f32[256,128]{1,0:T(8,128)S(1)} %collective-permute-done.10.piece), channel_id=1, source_target_pairs={{0,1},{1,0},{8,9},{9,8},{16,17},{17,16},{24,25},{25,24},{2,3},{3,2... | collective-permute-start | bytes 393224 | tf_op jit(solution)/shard_map/ppermute | solution.py:50

commit v5 on v4

--- a/solution.py
+++ b/solution.py
@@ -16,7 +16,7 @@
 N_PART = 4
 STEP = NB // N_PROW
 SLOTS = 32
-BLOCK = 16
+BLOCK = 32
 PLAN_ROWS = 8
 
 VMEM = pl.BlockSpec(memory_space=pltpu.VMEM)
@@ -120,18 +120,15 @@
     )(pivots)
 
 
-def pack_kernel(turn, plan_hbm, matrix, out, plan, held, top, moved, sems, row_sems, out_sems):
+def pack_kernel(turn, plan, matrix, out, held, top, moved, sem, row_sems, out_sems):
     my_row, _ = my_place()
     on_top = my_row == 0
-    load = pltpu.make_async_copy(plan_hbm, plan, sems.at[0])
-    load_top = pltpu.make_async_copy(matrix.at[pl.ds(0, NB), :], top, sems.at[1])
-    load.start()
+    load_top = pltpu.make_async_copy(matrix.at[pl.ds(0, NB), :], top, sem)
 
     @pl.when(on_top)
     def _():
         load_top.start()
 
-    load.wait()
     first = turn[0] * SLOTS
     copies = [
         pltpu.make_async_copy(
@@ -188,14 +185,13 @@
     return pl.pallas_call(
         pack_kernel,
         out_shape=jax.ShapeDtypeStruct((N_PROW, 2 * SLOTS, cols), jnp.float32),
-        in_specs=[SMEM, ANY, ANY],
+        in_specs=[SMEM, SMEM, ANY],
         out_specs=ANY,
         scratch_shapes=[
-            pltpu.SMEM((PLAN_ROWS, NB), jnp.int32),
             pltpu.VMEM((SLOTS, cols), jnp.float32),
             pltpu.VMEM((NB, cols), jnp.float32),
             pltpu.VMEM(((N_PROW + 1) * SLOTS, cols), jnp.float32),
-            pltpu.SemaphoreType.DMA((2,)),
+            pltpu.SemaphoreType.DMA,
             pltpu.SemaphoreType.DMA((SLOTS,)),
             pltpu.SemaphoreType.DMA((2 * N_PROW,)),
         ],
@@ -447,11 +443,12 @@
 def local(matrix, pivot_rows):
     zh, x, c = (lax.axis_index(name) for name in COLS)
     zl, y = (lax.axis_index(name) for name in ROWS)
-    panel = lax.optimization_barrier(matrix[:, :NB])
-    lower = panel[:NB]
+    lower = lax.optimization_barrier(matrix[:NB, :NB])
     targets = ((1, 0), (0, 1), (0, 3))
     received = [send_rows(lower, [((0, 0), t)], [0]) for t in targets]
     plan = make_plan(pivot_rows.reshape(1, NB))
+    panel = matrix[:, :NB]
+    panel, plan = lax.optimization_barrier((panel, plan))
     *received, plan = lax.optimization_barrier((*received, plan))
     for (a, b), got in zip(targets, received):
         lower = jnp.where((zl == a) & (y == b), got, lower)

time: 52.1 us -> 51.8 us (level)
  starting transfers between devices: 21.9 us -> 20.3 us
  Pallas kernels: 11.2 us -> 12.5 us
  waiting for transfers between devices: 15.2 us -> 14.2 us
  local copies, waits for them, and re-layouts: 2.22 us -> 3.06 us
    all_to_all x1, starting transfers between devices: 6.46 us -> 4.75 us  [local(): rows = lax.all_to_all(after(sent, lower), ROWS, 0, 0)]
    pallas_call x1, Pallas kernels: 3.33 us -> 4.76 us  [pack(): pl.pallas_call(pack_kernel, out_shape=jax.ShapeDtypeStruct((N_PROW, 2 * S...]
    ppermute x7, waiting for transfers between devices: 13.8 us -> 12.8 us  [send_cols(): lax.ppermute(value, COLS, [(pcol_id(*s), pcol_id(*t)) for s, t in pairs])]
    slice x2, local copies, waits for them, and re-layouts: 1.08 us -> 1.92 us  [the longest x1 1.08 us: local(): panel = matrix[:, :NB]]
  transfers between devices with their start and end apart: 14 -> 14, of which waited for: 3 -> 3; matrix products, arithmetic and copies ran while one was open for 1% -> 3% of each run, Pallas kernels for 19% -> 22%
where the time goes in v5:
time: 51.8 us; the launch traced here: 51.1 us
  starting transfers between devices  20.3 us (39%)
  waiting for transfers between devices  14.2 us (27%)
  Pallas kernels  12.5 us (24%)
  local copies, waits for them, and re-layouts  3.06 us (6%)
  loops' own time  0.55 us (1%)
    ppermute x7, waiting for transfers between devices, send_cols(): lax.ppermute(value, COLS, [(pcol_id(*s), pcol_id(*t)) for s, t in pairs])  12.8 us
    ppermute x7, starting transfers between devices, send_cols(): lax.ppermute(value, COLS, [(pcol_id(*s), pcol_id(*t)) for s, t in pairs])  10.3 us
    pallas_call x4, Pallas kernels, update(): pl.pallas_call(functools.partial(update_kernel, mine, late), out_shape=ja...  5.51 us
    pallas_call x1, Pallas kernels, pack(): pl.pallas_call(pack_kernel, out_shape=jax.ShapeDtypeStruct((N_PROW, 2 * S...  4.76 us
    all_to_all x1, starting transfers between devices, local(): rows = lax.all_to_all(after(sent, lower), ROWS, 0, 0)  4.75 us
    ppermute x4, starting transfers between devices, send_rows(): return lax.ppermute(value, ROWS + COLS, pairs)  2.65 us
    ppermute x2, starting transfers between devices, send_along_zh(): return lax.ppermute(value, ROWS + COLS, pairs)  2.59 us
    pallas_call x1, Pallas kernels, prepare(): pl.pallas_call(prepare_kernel, out_shape=(jax.ShapeDtypeStruct(matrix.sha...  2.01 us
  transfers between devices with their start and end apart: 14, of which 3 were waited for; matrix products, arithmetic and copies ran while one was open for 3% of the time, Pallas kernels for 22%

profile of v5, /device:TPU:1, one launch (start us, length us, event | category | flops | bytes accessed | tf_op | source)
XLA Modules:
  0.0 51.1 jit_solution(17289493101672482468)
XLA Ops:
  0.0 0.8 %slice.9 = f32[128,128]{1,0:T(8,128)S(1)} slice(f32[1024,768]{1,0:T(8,128)} %matrix.3), slice={[0:128], [0:128]} | slice | bytes 131072 | tf_op jit(solution)/shard_map/slice | solution.py:446
  0.8 0.7 %collective-permute-start.2 = (f32[128,128]{1,0:T(8,128)S(1)}, f32[128,128]{1,0:T(8,128)S(1)}, u32[]{:S(2)}, u32[]{:S(2)}) collective-permute-start(f32[128,128]{1,0:T(8,128)S(1)} %slice.9), channel_id=1, source_target_pairs={{0,96}} | collective-permute-start | bytes 196616 | tf_op jit(solution)/shard_map/ppermute | solution.py:55
  1.5 0.7 %collective-permute-start.1 = (f32[128,128]{1,0:T(8,128)S(1)}, f32[128,128]{1,0:T(8,128)S(1)}, u32[]{:S(2)}, u32[]{:S(2)}) collective-permute-start(f32[128,128]{1,0:T(8,128)S(1)} %slice.9), channel_id=1, source_target_pairs={{0,32}} | collective-permute-start | bytes 196616 | tf_op jit(solution)/shard_map/ppermute | solution.py:55
  2.2 0.7 %collective-permute-start = (f32[128,128]{1,0:T(8,128)S(1)}, f32[128,128]{1,0:T(8,128)S(1)}, u32[]{:S(2)}, u32[]{:S(2)}) collective-permute-start(f32[128,128]{1,0:T(8,128)S(1)} %slice.9), channel_id=1, source_target_pairs={{0,128}} | collective-permute-start | bytes 196616 | tf_op jit(solution)/shard_map/ppermute | solution.py:55
  2.9 1.1 %slice.10.panel_hbm = f32[1024,128]{1,0:T(8,128)S(1)} slice(f32[1024,768]{1,0:T(8,128)} %matrix.3), slice={[0:1024], [0:128]} | slice | bytes 1048576 | tf_op jit(solution)/shard_map/slice | solution.py:450
  4.9 0.7 %collective-permute-start.3 = (f32[128,128]{1,0:T(8,128)S(1)}, f32[128,128]{1,0:T(8,128)S(1)}, u32[]{:S(2)}, u32[]{:S(2)}) collective-permute-start(f32[128,128]{1,0:T(8,128)S(1)} %select_select_fusion.1), channel_id=1, source_target_pairs={{0,64},{128,192},{32,160},{96,224}} | collective-permute-start | bytes 196616 | tf_op jit(solution)/shard_map/ppermute | solution.py:55
  5.6 4.8 %pack.8 = f32[8,64,768]{2,1,0:T(8,128)} custom-call(s32[1]{0:T(128)} %constant.63.clone.1.turn, s32[8,128]{1,0:T(8,128)S(1)} %plan.1.plan_hbm, f32[1024,768]{1,0:T(8,128)} %matrix.3), custom_call_target="tpu_custom_call" | custom-call | bytes 6291456 | tf_op jit(solution)/shard_map/pack/pallas_call | solution.py:185
  10.4 4.8 %all-to-all-start.1 = ((f32[8,64,768]{2,1,0:T(8,128)}), f32[8,64,768]{2,1,0:T(8,128)S(1)}, u32[]{:S(2)}, u32[]{:S(2)}) async-start(f32[8,64,768]{2,1,0:T(8,128)} %pack.8), calls=%async_computation.1 | async-start | bytes 3145728 | tf_op jit(solution)/shard_map/all_to_all | solution.py:461
  15.2 0.7 %collective-permute-start.4 = (f32[256,128]{1,0:T(8,128)S(1)}, f32[256,128]{1,0:T(8,128)S(1)}, u32[]{:S(2)}, u32[]{:S(2)}) collective-permute-start(f32[256,128]{1,0:T(8,128)S(1)} %get-tuple-element.140), channel_id=1, source_target_pairs={{0,2},{32,34},{64,66},{96,98},{128,130},{160,162},{192,194},{224,2... | collective-permute-start | bytes 393224 | tf_op jit(solution)/shard_map/ppermute | solution.py:50
  15.8 0.7 %collective-permute-start.5 = (f32[256,128]{1,0:T(8,128)S(1)}, f32[256,128]{1,0:T(8,128)S(1)}, u32[]{:S(2)}, u32[]{:S(2)}) collective-permute-start(f32[256,128]{1,0:T(8,128)S(1)} %get-tuple-element.142), channel_id=1, source_target_pairs={{0,7},{32,39},{64,71},{96,103},{128,135},{160,167},{192,199},{224,... | collective-permute-start | bytes 393224 | tf_op jit(solution)/shard_map/ppermute | solution.py:50
  16.5 1.3 %collective-permute-start.6 = (f32[256,128]{1,0:T(8,128)S(1)}, f32[256,128]{1,0:T(8,128)S(1)}, u32[]{:S(2)}, u32[]{:S(2)}) collective-permute-start(f32[256,128]{1,0:T(8,128)S(1)} %get-tuple-element.143), channel_id=1, source_target_pairs={{0,1},{32,33},{64,65},{96,97},{128,129},{160,161},{192,193},{224,2... | collective-permute-start | bytes 393224 | tf_op jit(solution)/shard_map/ppermute | solution.py:50
  17.8 10.8 %collective-permute-done.6 = f32[256,128]{1,0:T(8,128)S(1)} collective-permute-done((f32[256,128]{1,0:T(8,128)S(1)}, f32[256,128]{1,0:T(8,128)S(1)}, u32[]{:S(2)}, u32[]{:S(2)}) %collective-permute-start.6) | collective-permute-done | bytes 131104 | tf_op jit(solution)/shard_map/ppermute | solution.py:50
  28.7 1.3 %collective-permute-start.7 = (f32[256,128]{1,0:T(8,128)S(1)}, f32[256,128]{1,0:T(8,128)S(1)}, u32[]{:S(2)}, u32[]{:S(2)}) collective-permute-start(f32[256,128]{1,0:T(8,128)S(1)} %select_select_fusion), channel_id=1, source_target_pairs={{0,6},{2,4},{1,3},{7,5},{32,38},{34,36},{33,35},{39,37},{64,70},{6... | collective-permute-start | bytes 393224 | tf_op jit(solution)/shard_map/ppermute | solution.py:50
  30.0 1.9 %collective-permute-done.7 = f32[256,128]{1,0:T(8,128)S(1)} collective-permute-done((f32[256,128]{1,0:T(8,128)S(1)}, f32[256,128]{1,0:T(8,128)S(1)}, u32[]{:S(2)}, u32[]{:S(2)}) %collective-permute-start.7) | collective-permute-done | bytes 131104 | tf_op jit(solution)/shard_map/ppermute | solution.py:50
  32.0 1.3 %collective-permute-start.8 = (f32[256,128]{1,0:T(8,128)S(1)}, f32[256,128]{1,0:T(8,128)S(1)}, u32[]{:S(2)}, u32[]{:S(2)}) collective-permute-start(f32[256,128]{1,0:T(8,128)S(1)} %broadcast_select_fusion), channel_id=1, source_target_pairs={{0,8},{1,25},{2,10},{3,27},{4,12},{5,29},{6,14},{7,31},{32,40},{33... | collective-permute-start | bytes 393224 | tf_op jit(solution)/shard_map/ppermute | solution.py:67
  33.8 1.4 %collective-permute-done.8 = f32[256,128]{1,0:T(8,128)S(1)} collective-permute-done((f32[256,128]{1,0:T(8,128)S(1)}, f32[256,128]{1,0:T(8,128)S(1)}, u32[]{:S(2)}, u32[]{:S(2)}) %collective-permute-start.8) | collective-permute-done | bytes 131104 | tf_op jit(solution)/shard_map/ppermute | solution.py:67
  35.2 1.3 %collective-permute-start.9 = (f32[256,128]{1,0:T(8,128)S(1)}, f32[256,128]{1,0:T(8,128)S(1)}, u32[]{:S(2)}, u32[]{:S(2)}) collective-permute-start(f32[256,128]{1,0:T(8,128)S(1)} %broadcast_select_fusion.1), channel_id=1, source_target_pairs={{0,24},{8,16},{1,9},{25,17},{2,26},{10,18},{3,11},{27,19},{4,28},{... | collective-permute-start | bytes 393224 | tf_op jit(solution)/shard_map/ppermute | solution.py:67
  37.1 2.0 %prepare.1 = (f32[1024,768]{1,0:T(8,128)S(1)}, bf16[3,256,768]{2,1,0:T(8,128)(2,1)S(1)}) custom-call(s32[8,128]{1,0:T(8,128)S(1)} %get-tuple-element.246, f32[8,64,768]{2,1,0:T(8,128)S(1)} %all-to-all-done.1.rows, f32[3,8,64,768]{3,2,1,0:T(8,128)} %get-tuple-element.148.rest, f32[1024,768]{1,0:T(8,128)} %get-tuple-element.233), custom_call_target="tpu_custom_call" | custom-call | bytes 9437184 | tf_op jit(solution)/shard_map/prepare/pallas_call | solution.py:355
  39.1 2.9 %collective-permute-start.11 = (f32[256,128]{1,0:T(8,128)S(1)}, f32[256,128]{1,0:T(8,128)S(1)}, u32[]{:S(2)}, u32[]{:S(2)}) collective-permute-start(f32[256,128]{1,0:T(8,128)S(1)} %broadcast_select_fusion.2.piece), channel_id=1, source_target_pairs={{0,1},{1,0},{8,9},{9,8},{16,17},{17,16},{24,25},{25,24},{2,3},{3,2... | collective-permute-start | bytes 393224 | tf_op jit(solution)/shard_map/ppermute | solution.py:50
  42.1 3.4 %collective-permute-start.10 = (f32[256,128]{1,0:T(8,128)S(1)}, f32[256,128]{1,0:T(8,128)S(1)}, u32[]{:S(2)}, u32[]{:S(2)}) collective-permute-start(f32[256,128]{1,0:T(8,128)S(1)} %broadcast_select_fusion.2.piece), channel_id=1, source_target_pairs={{0,2},{8,10},{16,18},{24,26},{2,0},{10,8},{18,16},{26,24},{4,6},{1... | collective-permute-start | bytes 393224 | tf_op jit(solution)/shard_map/ppermute | solution.py:50
  45.4 1.4 %update.4.refs_0_ = f32[1024,768]{1,0:T(8,128)} custom-call(f32[256,128]{1,0:T(8,128)S(1)} %broadcast_select_fusion.2.piece, bf16[3,256,768]{2,1,0:T(8,128)(2,1)S(1)} %get-tuple-element.149.factors, f32[1024,768]{1,0:T(8,128)S(1)} %get-tuple-element.151.base), custom_call_target="tpu_custom_call" | custom-call | bytes 2097152 | tf_op jit(solution)/shard_map/update/pallas_call | solution.py:403
  46.8 1.4 %update.5.refs_0_ = f32[1024,768]{1,0:T(8,128)} custom-call(f32[256,128]{1,0:T(8,128)S(1)} %collective-permute-done.11.piece, bf16[3,256,768]{2,1,0:T(8,128)(2,1)S(1)} %get-tuple-element.149.factors, f32[1024,768]{1,0:T(8,128)S(1)} %get-tuple-element.151.base, f32[1024,768]{1,0:T(8,128)} %update.4.refs_0_), custom_call_target="tpu_custom_call", output_to_operand_aliasing={{}: (3, {})} | custom-call | bytes 2097152 | tf_op jit(solution)/shard_map/update/pallas_call | solution.py:403
  48.3 1.4 %update.6.refs_0_ = f32[1024,768]{1,0:T(8,128)} custom-call(f32[256,128]{1,0:T(8,128)S(1)} %collective-permute-done.10.piece, bf16[3,256,768]{2,1,0:T(8,128)(2,1)S(1)} %get-tuple-element.149.factors, f32[1024,768]{1,0:T(8,128)S(1)} %get-tuple-element.151.base, f32[1024,768]{1,0:T(8,128)} %update.5.refs_0_), custom_call_target="tpu_custom_call", output_to_operand_aliasing={{}: (3, {})} | custom-call | bytes 2097152 | tf_op jit(solution)/shard_map/update/pallas_call | solution.py:403
  49.7 1.4 %update.7 = f32[1024,768]{1,0:T(8,128)} custom-call(f32[256,128]{1,0:T(8,128)S(1)} %collective-permute-done.12.piece, bf16[3,256,768]{2,1,0:T(8,128)(2,1)S(1)} %get-tuple-element.149.factors, f32[1024,768]{1,0:T(8,128)S(1)} %get-tuple-element.151.base, f32[1024,768]{1,0:T(8,128)} %update.6.refs_0_), custom_call_target="tpu_custom_call", output_to_operand_aliasing={{}: (3, {})} | custom-call | bytes 2097152 | tf_op jit(solution)/shard_map/update/pallas_call | solution.py:403
  (25 shorter events, 2.2 us)
Async XLA Ops:
  0.8 4.0 %collective-permute-start.2 = (f32[128,128]{1,0:T(8,128)S(1)}, f32[128,128]{1,0:T(8,128)S(1)}, u32[]{:S(2)}, u32[]{:S(2)}) collective-permute-start(f32[128,128]{1,0:T(8,128)S(1)} %slice.9), channel_id=1, source_target_pairs={{0,96}} | collective-permute-start | bytes 196616 | tf_op jit(solution)/shard_map/ppermute | solution.py:55
  1.5 3.4 %collective-permute-start.1 = (f32[128,128]{1,0:T(8,128)S(1)}, f32[128,128]{1,0:T(8,128)S(1)}, u32[]{:S(2)}, u32[]{:S(2)}) collective-permute-start(f32[128,128]{1,0:T(8,128)S(1)} %slice.9), channel_id=1, source_target_pairs={{0,32}} | collective-permute-start | bytes 196616 | tf_op jit(solution)/shard_map/ppermute | solution.py:55
  2.2 2.7 %collective-permute-start = (f32[128,128]{1,0:T(8,128)S(1)}, f32[128,128]{1,0:T(8,128)S(1)}, u32[]{:S(2)}, u32[]{:S(2)}) collective-permute-start(f32[128,128]{1,0:T(8,128)S(1)} %slice.9), channel_id=1, source_target_pairs={{0,128}} | collective-permute-start | bytes 196616 | tf_op jit(solution)/shard_map/ppermute | solution.py:55
  4.0 0.7 %copy-start = (s32[128]{0:T(128)S(1)}, s32[128]{0:T(128)}, u32[]{:S(2)}) copy-start(s32[128]{0:T(128)} %param.5) | copy-start | bytes 1540
  4.9 5.5 %collective-permute-start.3 = (f32[128,128]{1,0:T(8,128)S(1)}, f32[128,128]{1,0:T(8,128)S(1)}, u32[]{:S(2)}, u32[]{:S(2)}) collective-permute-start(f32[128,128]{1,0:T(8,128)S(1)} %select_select_fusion.1), channel_id=1, source_target_pairs={{0,64},{128,192},{32,160},{96,224}} | collective-permute-start | bytes 196616 | tf_op jit(solution)/shard_map/ppermute | solution.py:55
  10.4 26.1 %all-to-all-start.1 = ((f32[8,64,768]{2,1,0:T(8,128)}), f32[8,64,768]{2,1,0:T(8,128)S(1)}, u32[]{:S(2)}, u32[]{:S(2)}) async-start(f32[8,64,768]{2,1,0:T(8,128)} %pack.8), calls=%async_computation.1 | async-start | bytes 3145728 | tf_op jit(solution)/shard_map/all_to_all | solution.py:461
  15.2 2.7 %collective-permute-start.4 = (f32[256,128]{1,0:T(8,128)S(1)}, f32[256,128]{1,0:T(8,128)S(1)}, u32[]{:S(2)}, u32[]{:S(2)}) collective-permute-start(f32[256,128]{1,0:T(8,128)S(1)} %get-tuple-element.140), channel_id=1, source_target_pairs={{0,2},{32,34},{64,66},{96,98},{128,130},{160,162},{192,194},{224,2... | collective-permute-start | bytes 393224 | tf_op jit(solution)/shard_map/ppermute | solution.py:50
  15.8 2.0 %collective-permute-start.5 = (f32[256,128]{1,0:T(8,128)S(1)}, f32[256,128]{1,0:T(8,128)S(1)}, u32[]{:S(2)}, u32[]{:S(2)}) collective-permute-start(f32[256,128]{1,0:T(8,128)S(1)} %get-tuple-element.142), channel_id=1, source_target_pairs={{0,7},{32,39},{64,71},{96,103},{128,135},{160,167},{192,199},{224,... | collective-permute-start | bytes 393224 | tf_op jit(solution)/shard_map/ppermute | solution.py:50
  16.5 12.2 %collective-permute-start.6 = (f32[256,128]{1,0:T(8,128)S(1)}, f32[256,128]{1,0:T(8,128)S(1)}, u32[]{:S(2)}, u32[]{:S(2)}) collective-permute-start(f32[256,128]{1,0:T(8,128)S(1)} %get-tuple-element.143), channel_id=1, source_target_pairs={{0,1},{32,33},{64,65},{96,97},{128,129},{160,161},{192,193},{224,2... | collective-permute-start | bytes 393224 | tf_op jit(solution)/shard_map/ppermute | solution.py:50
  28.7 3.2 %collective-permute-start.7 = (f32[256,128]{1,0:T(8,128)S(1)}, f32[256,128]{1,0:T(8,128)S(1)}, u32[]{:S(2)}, u32[]{:S(2)}) collective-permute-start(f32[256,128]{1,0:T(8,128)S(1)} %select_select_fusion), channel_id=1, source_target_pairs={{0,6},{2,4},{1,3},{7,5},{32,38},{34,36},{33,35},{39,37},{64,70},{6... | collective-permute-start | bytes 393224 | tf_op jit(solution)/shard_map/ppermute | solution.py:50
  32.0 3.2 %collective-permute-start.8 = (f32[256,128]{1,0:T(8,128)S(1)}, f32[256,128]{1,0:T(8,128)S(1)}, u32[]{:S(2)}, u32[]{:S(2)}) collective-permute-start(f32[256,128]{1,0:T(8,128)S(1)} %broadcast_select_fusion), channel_id=1, source_target_pairs={{0,8},{1,25},{2,10},{3,27},{4,12},{5,29},{6,14},{7,31},{32,40},{33... | collective-permute-start | bytes 393224 | tf_op jit(solution)/shard_map/ppermute | solution.py:67
  35.2 3.9 %collective-permute-start.9 = (f32[256,128]{1,0:T(8,128)S(1)}, f32[256,128]{1,0:T(8,128)S(1)}, u32[]{:S(2)}, u32[]{:S(2)}) collective-permute-start(f32[256,128]{1,0:T(8,128)S(1)} %broadcast_select_fusion.1), channel_id=1, source_target_pairs={{0,24},{8,16},{1,9},{25,17},{2,26},{10,18},{3,11},{27,19},{4,28},{... | collective-permute-start | bytes 393224 | tf_op jit(solution)/shard_map/ppermute | solution.py:67
  39.1 7.7 %collective-permute-start.11 = (f32[256,128]{1,0:T(8,128)S(1)}, f32[256,128]{1,0:T(8,128)S(1)}, u32[]{:S(2)}, u32[]{:S(2)}) collective-permute-start(f32[256,128]{1,0:T(8,128)S(1)} %broadcast_select_fusion.2.piece), channel_id=1, source_target_pairs={{0,1},{1,0},{8,9},{9,8},{16,17},{17,16},{24,25},{25,24},{2,3},{3,2... | collective-permute-start | bytes 393224 | tf_op jit(solution)/shard_map/ppermute | solution.py:50
  42.1 6.2 %collective-permute-start.10 = (f32[256,128]{1,0:T(8,128)S(1)}, f32[256,128]{1,0:T(8,128)S(1)}, u32[]{:S(2)}, u32[]{:S(2)}) collective-permute-start(f32[256,128]{1,0:T(8,128)S(1)} %broadcast_select_fusion.2.piece), channel_id=1, source_target_pairs={{0,2},{8,10},{16,18},{24,26},{2,0},{10,8},{18,16},{26,24},{4,6},{1... | collective-permute-start | bytes 393224 | tf_op jit(solution)/shard_map/ppermute | solution.py:50
  48.2 1.5 %collective-permute-start.12 = (f32[256,128]{1,0:T(8,128)S(1)}, f32[256,128]{1,0:T(8,128)S(1)}, u32[]{:S(2)}, u32[]{:S(2)}) collective-permute-start(f32[256,128]{1,0:T(8,128)S(1)} %collective-permute-done.10.piece), channel_id=1, source_target_pairs={{0,1},{1,0},{8,9},{9,8},{16,17},{17,16},{24,25},{25,24},{2,3},{3,2... | collective-permute-start | bytes 393224 | tf_op jit(solution)/shard_map/ppermute | solution.py:50

commit v6 on v5

--- a/solution.py
+++ b/solution.py
@@ -444,7 +444,7 @@
     zh, x, c = (lax.axis_index(name) for name in COLS)
     zl, y = (lax.axis_index(name) for name in ROWS)
     lower = lax.optimization_barrier(matrix[:NB, :NB])
-    targets = ((1, 0), (0, 1), (0, 3))
+    targets = ((0, 3), (0, 1), (1, 0))
     received = [send_rows(lower, [((0, 0), t)], [0]) for t in targets]
     plan = make_plan(pivot_rows.reshape(1, NB))
     panel = matrix[:, :NB]

time: 51.8 us -> 50.3 us (0.971)
  waiting for transfers between devices: 14.2 us -> 12.8 us
    ppermute x7, waiting for transfers between devices: 12.8 us -> 11.3 us  [send_cols(): lax.ppermute(value, COLS, [(pcol_id(*s), pcol_id(*t)) for s, t in pairs])]
where the time goes in v6:
time: 50.3 us; the launch traced here: 49.8 us
  starting transfers between devices  20.4 us (41%)
  waiting for transfers between devices  12.8 us (25%)
  Pallas kernels  12.6 us (25%)
  local copies, waits for them, and re-layouts  3.06 us (6%)
  loops' own time  0.55 us (1%)
    ppermute x7, waiting for transfers between devices, send_cols(): lax.ppermute(value, COLS, [(pcol_id(*s), pcol_id(*t)) for s, t in pairs])  11.3 us
    ppermute x7, starting transfers between devices, send_cols(): lax.ppermute(value, COLS, [(pcol_id(*s), pcol_id(*t)) for s, t in pairs])  10.3 us
    pallas_call x4, Pallas kernels, update(): pl.pallas_call(functools.partial(update_kernel, mine, late), out_shape=ja...  5.51 us
    pallas_call x1, Pallas kernels, pack(): pl.pallas_call(pack_kernel, out_shape=jax.ShapeDtypeStruct((N_PROW, 2 * S...  4.82 us
    all_to_all x1, starting transfers between devices, local(): rows = lax.all_to_all(after(sent, lower), ROWS, 0, 0)  4.81 us
    ppermute x4, starting transfers between devices, send_rows(): return lax.ppermute(value, ROWS + COLS, pairs)  2.65 us
    ppermute x2, starting transfers between devices, send_along_zh(): return lax.ppermute(value, ROWS + COLS, pairs)  2.59 us
    pallas_call x1, Pallas kernels, prepare(): pl.pallas_call(prepare_kernel, out_shape=(jax.ShapeDtypeStruct(matrix.sha...  1.99 us
  transfers between devices with their start and end apart: 14, of which 3 were waited for; matrix products, arithmetic and copies ran while one was open for 3% of the time, Pallas kernels for 22%

profile of v6, /device:TPU:1, one launch (start us, length us, event | category | flops | bytes accessed | tf_op | source)
XLA Modules:
  0.0 49.8 jit_solution(245468981523345157)
XLA Ops:
  0.0 0.8 %slice.9 = f32[128,128]{1,0:T(8,128)S(1)} slice(f32[1024,768]{1,0:T(8,128)} %matrix.3), slice={[0:128], [0:128]} | slice | bytes 131072 | tf_op jit(solution)/shard_map/slice | solution.py:446
  0.8 0.7 %collective-permute-start.2 = (f32[128,128]{1,0:T(8,128)S(1)}, f32[128,128]{1,0:T(8,128)S(1)}, u32[]{:S(2)}, u32[]{:S(2)}) collective-permute-start(f32[128,128]{1,0:T(8,128)S(1)} %slice.9), channel_id=1, source_target_pairs={{0,128}} | collective-permute-start | bytes 196616 | tf_op jit(solution)/shard_map/ppermute | solution.py:55
  1.5 0.7 %collective-permute-start.1 = (f32[128,128]{1,0:T(8,128)S(1)}, f32[128,128]{1,0:T(8,128)S(1)}, u32[]{:S(2)}, u32[]{:S(2)}) collective-permute-start(f32[128,128]{1,0:T(8,128)S(1)} %slice.9), channel_id=1, source_target_pairs={{0,32}} | collective-permute-start | bytes 196616 | tf_op jit(solution)/shard_map/ppermute | solution.py:55
  2.2 0.7 %collective-permute-start = (f32[128,128]{1,0:T(8,128)S(1)}, f32[128,128]{1,0:T(8,128)S(1)}, u32[]{:S(2)}, u32[]{:S(2)}) collective-permute-start(f32[128,128]{1,0:T(8,128)S(1)} %slice.9), channel_id=1, source_target_pairs={{0,96}} | collective-permute-start | bytes 196616 | tf_op jit(solution)/shard_map/ppermute | solution.py:55
  2.9 1.1 %slice.10.panel_hbm = f32[1024,128]{1,0:T(8,128)S(1)} slice(f32[1024,768]{1,0:T(8,128)} %matrix.3), slice={[0:1024], [0:128]} | slice | bytes 1048576 | tf_op jit(solution)/shard_map/slice | solution.py:450
  4.9 0.7 %collective-permute-start.3 = (f32[128,128]{1,0:T(8,128)S(1)}, f32[128,128]{1,0:T(8,128)S(1)}, u32[]{:S(2)}, u32[]{:S(2)}) collective-permute-start(f32[128,128]{1,0:T(8,128)S(1)} %select_select_fusion.1), channel_id=1, source_target_pairs={{0,64},{128,192},{32,160},{96,224}} | collective-permute-start | bytes 196616 | tf_op jit(solution)/shard_map/ppermute | solution.py:55
  5.6 4.8 %pack.8 = f32[8,64,768]{2,1,0:T(8,128)} custom-call(s32[1]{0:T(128)} %constant.63.clone.1.turn, s32[8,128]{1,0:T(8,128)S(1)} %plan.1.plan_hbm, f32[1024,768]{1,0:T(8,128)} %matrix.3), custom_call_target="tpu_custom_call" | custom-call | bytes 6291456 | tf_op jit(solution)/shard_map/pack/pallas_call | solution.py:185
  10.4 4.8 %all-to-all-start.1 = ((f32[8,64,768]{2,1,0:T(8,128)}), f32[8,64,768]{2,1,0:T(8,128)S(1)}, u32[]{:S(2)}, u32[]{:S(2)}) async-start(f32[8,64,768]{2,1,0:T(8,128)} %pack.8), calls=%async_computation.1 | async-start | bytes 3145728 | tf_op jit(solution)/shard_map/all_to_all | solution.py:461
  15.3 0.7 %collective-permute-start.4 = (f32[256,128]{1,0:T(8,128)S(1)}, f32[256,128]{1,0:T(8,128)S(1)}, u32[]{:S(2)}, u32[]{:S(2)}) collective-permute-start(f32[256,128]{1,0:T(8,128)S(1)} %get-tuple-element.140), channel_id=1, source_target_pairs={{0,2},{32,34},{64,66},{96,98},{128,130},{160,162},{192,194},{224,2... | collective-permute-start | bytes 393224 | tf_op jit(solution)/shard_map/ppermute | solution.py:50
  16.0 0.7 %collective-permute-start.5 = (f32[256,128]{1,0:T(8,128)S(1)}, f32[256,128]{1,0:T(8,128)S(1)}, u32[]{:S(2)}, u32[]{:S(2)}) collective-permute-start(f32[256,128]{1,0:T(8,128)S(1)} %get-tuple-element.142), channel_id=1, source_target_pairs={{0,7},{32,39},{64,71},{96,103},{128,135},{160,167},{192,199},{224,... | collective-permute-start | bytes 393224 | tf_op jit(solution)/shard_map/ppermute | solution.py:50
  16.6 1.3 %collective-permute-start.6 = (f32[256,128]{1,0:T(8,128)S(1)}, f32[256,128]{1,0:T(8,128)S(1)}, u32[]{:S(2)}, u32[]{:S(2)}) collective-permute-start(f32[256,128]{1,0:T(8,128)S(1)} %get-tuple-element.143), channel_id=1, source_target_pairs={{0,1},{32,33},{64,65},{96,97},{128,129},{160,161},{192,193},{224,2... | collective-permute-start | bytes 393224 | tf_op jit(solution)/shard_map/ppermute | solution.py:50
  18.0 9.4 %collective-permute-done.6 = f32[256,128]{1,0:T(8,128)S(1)} collective-permute-done((f32[256,128]{1,0:T(8,128)S(1)}, f32[256,128]{1,0:T(8,128)S(1)}, u32[]{:S(2)}, u32[]{:S(2)}) %collective-permute-start.6) | collective-permute-done | bytes 131104 | tf_op jit(solution)/shard_map/ppermute | solution.py:50
  27.4 1.3 %collective-permute-start.7 = (f32[256,128]{1,0:T(8,128)S(1)}, f32[256,128]{1,0:T(8,128)S(1)}, u32[]{:S(2)}, u32[]{:S(2)}) collective-permute-start(f32[256,128]{1,0:T(8,128)S(1)} %select_select_fusion), channel_id=1, source_target_pairs={{0,6},{2,4},{1,3},{7,5},{32,38},{34,36},{33,35},{39,37},{64,70},{6... | collective-permute-start | bytes 393224 | tf_op jit(solution)/shard_map/ppermute | solution.py:50
  28.7 1.9 %collective-permute-done.7 = f32[256,128]{1,0:T(8,128)S(1)} collective-permute-done((f32[256,128]{1,0:T(8,128)S(1)}, f32[256,128]{1,0:T(8,128)S(1)}, u32[]{:S(2)}, u32[]{:S(2)}) %collective-permute-start.7) | collective-permute-done | bytes 131104 | tf_op jit(solution)/shard_map/ppermute | solution.py:50
  30.7 1.3 %collective-permute-start.8 = (f32[256,128]{1,0:T(8,128)S(1)}, f32[256,128]{1,0:T(8,128)S(1)}, u32[]{:S(2)}, u32[]{:S(2)}) collective-permute-start(f32[256,128]{1,0:T(8,128)S(1)} %broadcast_select_fusion), channel_id=1, source_target_pairs={{0,8},{1,25},{2,10},{3,27},{4,12},{5,29},{6,14},{7,31},{32,40},{33... | collective-permute-start | bytes 393224 | tf_op jit(solution)/shard_map/ppermute | solution.py:67
  32.5 1.4 %collective-permute-done.8 = f32[256,128]{1,0:T(8,128)S(1)} collective-permute-done((f32[256,128]{1,0:T(8,128)S(1)}, f32[256,128]{1,0:T(8,128)S(1)}, u32[]{:S(2)}, u32[]{:S(2)}) %collective-permute-start.8) | collective-permute-done | bytes 131104 | tf_op jit(solution)/shard_map/ppermute | solution.py:67
  33.9 1.3 %collective-permute-start.9 = (f32[256,128]{1,0:T(8,128)S(1)}, f32[256,128]{1,0:T(8,128)S(1)}, u32[]{:S(2)}, u32[]{:S(2)}) collective-permute-start(f32[256,128]{1,0:T(8,128)S(1)} %broadcast_select_fusion.1), channel_id=1, source_target_pairs={{0,24},{8,16},{1,9},{25,17},{2,26},{10,18},{3,11},{27,19},{4,28},{... | collective-permute-start | bytes 393224 | tf_op jit(solution)/shard_map/ppermute | solution.py:67
  35.8 2.0 %prepare.1 = (f32[1024,768]{1,0:T(8,128)S(1)}, bf16[3,256,768]{2,1,0:T(8,128)(2,1)S(1)}) custom-call(s32[8,128]{1,0:T(8,128)S(1)} %get-tuple-element.246, f32[8,64,768]{2,1,0:T(8,128)S(1)} %all-to-all-done.1.rows, f32[3,8,64,768]{3,2,1,0:T(8,128)} %get-tuple-element.148.rest, f32[1024,768]{1,0:T(8,128)} %get-tuple-element.233), custom_call_target="tpu_custom_call" | custom-call | bytes 9437184 | tf_op jit(solution)/shard_map/prepare/pallas_call | solution.py:355
  37.8 2.9 %collective-permute-start.11 = (f32[256,128]{1,0:T(8,128)S(1)}, f32[256,128]{1,0:T(8,128)S(1)}, u32[]{:S(2)}, u32[]{:S(2)}) collective-permute-start(f32[256,128]{1,0:T(8,128)S(1)} %broadcast_select_fusion.2.piece), channel_id=1, source_target_pairs={{0,1},{1,0},{8,9},{9,8},{16,17},{17,16},{24,25},{25,24},{2,3},{3,2... | collective-permute-start | bytes 393224 | tf_op jit(solution)/shard_map/ppermute | solution.py:50
  40.8 3.4 %collective-permute-start.10 = (f32[256,128]{1,0:T(8,128)S(1)}, f32[256,128]{1,0:T(8,128)S(1)}, u32[]{:S(2)}, u32[]{:S(2)}) collective-permute-start(f32[256,128]{1,0:T(8,128)S(1)} %broadcast_select_fusion.2.piece), channel_id=1, source_target_pairs={{0,2},{8,10},{16,18},{24,26},{2,0},{10,8},{18,16},{26,24},{4,6},{1... | collective-permute-start | bytes 393224 | tf_op jit(solution)/shard_map/ppermute | solution.py:50
  44.1 1.4 %update.4.refs_0_ = f32[1024,768]{1,0:T(8,128)} custom-call(f32[256,128]{1,0:T(8,128)S(1)} %broadcast_select_fusion.2.piece, bf16[3,256,768]{2,1,0:T(8,128)(2,1)S(1)} %get-tuple-element.149.factors, f32[1024,768]{1,0:T(8,128)S(1)} %get-tuple-element.151.base), custom_call_target="tpu_custom_call" | custom-call | bytes 2097152 | tf_op jit(solution)/shard_map/update/pallas_call | solution.py:403
  45.5 1.4 %update.5.refs_0_ = f32[1024,768]{1,0:T(8,128)} custom-call(f32[256,128]{1,0:T(8,128)S(1)} %collective-permute-done.11.piece, bf16[3,256,768]{2,1,0:T(8,128)(2,1)S(1)} %get-tuple-element.149.factors, f32[1024,768]{1,0:T(8,128)S(1)} %get-tuple-element.151.base, f32[1024,768]{1,0:T(8,128)} %update.4.refs_0_), custom_call_target="tpu_custom_call", output_to_operand_aliasing={{}: (3, {})} | custom-call | bytes 2097152 | tf_op jit(solution)/shard_map/update/pallas_call | solution.py:403
  47.0 1.4 %update.6.refs_0_ = f32[1024,768]{1,0:T(8,128)} custom-call(f32[256,128]{1,0:T(8,128)S(1)} %collective-permute-done.10.piece, bf16[3,256,768]{2,1,0:T(8,128)(2,1)S(1)} %get-tuple-element.149.factors, f32[1024,768]{1,0:T(8,128)S(1)} %get-tuple-element.151.base, f32[1024,768]{1,0:T(8,128)} %update.5.refs_0_), custom_call_target="tpu_custom_call", output_to_operand_aliasing={{}: (3, {})} | custom-call | bytes 2097152 | tf_op jit(solution)/shard_map/update/pallas_call | solution.py:403
  48.4 1.4 %update.7 = f32[1024,768]{1,0:T(8,128)} custom-call(f32[256,128]{1,0:T(8,128)S(1)} %collective-permute-done.12.piece, bf16[3,256,768]{2,1,0:T(8,128)(2,1)S(1)} %get-tuple-element.149.factors, f32[1024,768]{1,0:T(8,128)S(1)} %get-tuple-element.151.base, f32[1024,768]{1,0:T(8,128)} %update.6.refs_0_), custom_call_target="tpu_custom_call", output_to_operand_aliasing={{}: (3, {})} | custom-call | bytes 2097152 | tf_op jit(solution)/shard_map/update/pallas_call | solution.py:403
  (25 shorter events, 2.2 us)
Async XLA Ops:
  0.8 4.0 %collective-permute-start.2 = (f32[128,128]{1,0:T(8,128)S(1)}, f32[128,128]{1,0:T(8,128)S(1)}, u32[]{:S(2)}, u32[]{:S(2)}) collective-permute-start(f32[128,128]{1,0:T(8,128)S(1)} %slice.9), channel_id=1, source_target_pairs={{0,128}} | collective-permute-start | bytes 196616 | tf_op jit(solution)/shard_map/ppermute | solution.py:55
  1.5 3.4 %collective-permute-start.1 = (f32[128,128]{1,0:T(8,128)S(1)}, f32[128,128]{1,0:T(8,128)S(1)}, u32[]{:S(2)}, u32[]{:S(2)}) collective-permute-start(f32[128,128]{1,0:T(8,128)S(1)} %slice.9), channel_id=1, source_target_pairs={{0,32}} | collective-permute-start | bytes 196616 | tf_op jit(solution)/shard_map/ppermute | solution.py:55
  2.2 2.7 %collective-permute-start = (f32[128,128]{1,0:T(8,128)S(1)}, f32[128,128]{1,0:T(8,128)S(1)}, u32[]{:S(2)}, u32[]{:S(2)}) collective-permute-start(f32[128,128]{1,0:T(8,128)S(1)} %slice.9), channel_id=1, source_target_pairs={{0,96}} | collective-permute-start | bytes 196616 | tf_op jit(solution)/shard_map/ppermute | solution.py:55
  4.0 0.7 %copy-start = (s32[128]{0:T(128)S(1)}, s32[128]{0:T(128)}, u32[]{:S(2)}) copy-start(s32[128]{0:T(128)} %param.5) | copy-start | bytes 1540
  4.9 5.5 %collective-permute-start.3 = (f32[128,128]{1,0:T(8,128)S(1)}, f32[128,128]{1,0:T(8,128)S(1)}, u32[]{:S(2)}, u32[]{:S(2)}) collective-permute-start(f32[128,128]{1,0:T(8,128)S(1)} %select_select_fusion.1), channel_id=1, source_target_pairs={{0,64},{128,192},{32,160},{96,224}} | collective-permute-start | bytes 196616 | tf_op jit(solution)/shard_map/ppermute | solution.py:55
  10.4 24.8 %all-to-all-start.1 = ((f32[8,64,768]{2,1,0:T(8,128)}), f32[8,64,768]{2,1,0:T(8,128)S(1)}, u32[]{:S(2)}, u32[]{:S(2)}) async-start(f32[8,64,768]{2,1,0:T(8,128)} %pack.8), calls=%async_computation.1 | async-start | bytes 3145728 | tf_op jit(solution)/shard_map/all_to_all | solution.py:461
  15.3 2.7 %collective-permute-start.4 = (f32[256,128]{1,0:T(8,128)S(1)}, f32[256,128]{1,0:T(8,128)S(1)}, u32[]{:S(2)}, u32[]{:S(2)}) collective-permute-start(f32[256,128]{1,0:T(8,128)S(1)} %get-tuple-element.140), channel_id=1, source_target_pairs={{0,2},{32,34},{64,66},{96,98},{128,130},{160,162},{192,194},{224,2... | collective-permute-start | bytes 393224 | tf_op jit(solution)/shard_map/ppermute | solution.py:50
  16.0 2.0 %collective-permute-start.5 = (f32[256,128]{1,0:T(8,128)S(1)}, f32[256,128]{1,0:T(8,128)S(1)}, u32[]{:S(2)}, u32[]{:S(2)}) collective-permute-start(f32[256,128]{1,0:T(8,128)S(1)} %get-tuple-element.142), channel_id=1, source_target_pairs={{0,7},{32,39},{64,71},{96,103},{128,135},{160,167},{192,199},{224,... | collective-permute-start | bytes 393224 | tf_op jit(solution)/shard_map/ppermute | solution.py:50
  16.6 10.8 %collective-permute-start.6 = (f32[256,128]{1,0:T(8,128)S(1)}, f32[256,128]{1,0:T(8,128)S(1)}, u32[]{:S(2)}, u32[]{:S(2)}) collective-permute-start(f32[256,128]{1,0:T(8,128)S(1)} %get-tuple-element.143), channel_id=1, source_target_pairs={{0,1},{32,33},{64,65},{96,97},{128,129},{160,161},{192,193},{224,2... | collective-permute-start | bytes 393224 | tf_op jit(solution)/shard_map/ppermute | solution.py:50
  27.4 3.2 %collective-permute-start.7 = (f32[256,128]{1,0:T(8,128)S(1)}, f32[256,128]{1,0:T(8,128)S(1)}, u32[]{:S(2)}, u32[]{:S(2)}) collective-permute-start(f32[256,128]{1,0:T(8,128)S(1)} %select_select_fusion), channel_id=1, source_target_pairs={{0,6},{2,4},{1,3},{7,5},{32,38},{34,36},{33,35},{39,37},{64,70},{6... | collective-permute-start | bytes 393224 | tf_op jit(solution)/shard_map/ppermute | solution.py:50
  30.7 3.2 %collective-permute-start.8 = (f32[256,128]{1,0:T(8,128)S(1)}, f32[256,128]{1,0:T(8,128)S(1)}, u32[]{:S(2)}, u32[]{:S(2)}) collective-permute-start(f32[256,128]{1,0:T(8,128)S(1)} %broadcast_select_fusion), channel_id=1, source_target_pairs={{0,8},{1,25},{2,10},{3,27},{4,12},{5,29},{6,14},{7,31},{32,40},{33... | collective-permute-start | bytes 393224 | tf_op jit(solution)/shard_map/ppermute | solution.py:67
  33.9 3.9 %collective-permute-start.9 = (f32[256,128]{1,0:T(8,128)S(1)}, f32[256,128]{1,0:T(8,128)S(1)}, u32[]{:S(2)}, u32[]{:S(2)}) collective-permute-start(f32[256,128]{1,0:T(8,128)S(1)} %broadcast_select_fusion.1), channel_id=1, source_target_pairs={{0,24},{8,16},{1,9},{25,17},{2,26},{10,18},{3,11},{27,19},{4,28},{... | collective-permute-start | bytes 393224 | tf_op jit(solution)/shard_map/ppermute | solution.py:67
  37.8 7.7 %collective-permute-start.11 = (f32[256,128]{1,0:T(8,128)S(1)}, f32[256,128]{1,0:T(8,128)S(1)}, u32[]{:S(2)}, u32[]{:S(2)}) collective-permute-start(f32[256,128]{1,0:T(8,128)S(1)} %broadcast_select_fusion.2.piece), channel_id=1, source_target_pairs={{0,1},{1,0},{8,9},{9,8},{16,17},{17,16},{24,25},{25,24},{2,3},{3,2... | collective-permute-start | bytes 393224 | tf_op jit(solution)/shard_map/ppermute | solution.py:50
  40.8 6.2 %collective-permute-start.10 = (f32[256,128]{1,0:T(8,128)S(1)}, f32[256,128]{1,0:T(8,128)S(1)}, u32[]{:S(2)}, u32[]{:S(2)}) collective-permute-start(f32[256,128]{1,0:T(8,128)S(1)} %broadcast_select_fusion.2.piece), channel_id=1, source_target_pairs={{0,2},{8,10},{16,18},{24,26},{2,0},{10,8},{18,16},{26,24},{4,6},{1... | collective-permute-start | bytes 393224 | tf_op jit(solution)/shard_map/ppermute | solution.py:50
  46.9 1.5 %collective-permute-start.12 = (f32[256,128]{1,0:T(8,128)S(1)}, f32[256,128]{1,0:T(8,128)S(1)}, u32[]{:S(2)}, u32[]{:S(2)}) collective-permute-start(f32[256,128]{1,0:T(8,128)S(1)} %collective-permute-done.10.piece), channel_id=1, source_target_pairs={{0,1},{1,0},{8,9},{9,8},{16,17},{17,16},{24,25},{25,24},{2,3},{3,2... | collective-permute-start | bytes 393224 | tf_op jit(solution)/shard_map/ppermute | solution.py:50
